TPU v7x, 32 devices: a whole 2x2x4 slice. The times are simulated.
32 devices in a mesh: dp: 16 (over z, y, core), ctx: 2 (over x).
Axes of the slice: x: 2, y: 2, z: 4, core: 2. Of those that a mesh axis runs over, the one named last changes fastest.
Arguments:
- tokens: bfloat16 [16, 1024, 768], P('dp', 'ctx'), may hold values from -6 to 6
- w_query: bfloat16 [768, 768], P('dp'), may hold values from -0.21875 to 0.21875
- w_key: bfloat16 [768, 768], P('dp'), may hold values from -0.21875 to 0.21875
- w_value: bfloat16 [768, 768], P('dp'), may hold values from -0.21875 to 0.21875
- w_out: bfloat16 [768, 768], P('dp')
- w_up: bfloat16 [768, 3072], P('dp'), may hold values from -0.21875 to 0.21875
- w_down: bfloat16 [3072, 768], P('dp'), may hold values from -0.109375 to 0.109375
- gain_attn: bfloat16 [768], P('dp'), may hold values from 0.5 to 1.5
- gain_ffn: bfloat16 [768], P('dp'), may hold values from 0.5 to 1.5
- teacher: bfloat16 [16, 1024, 768], P('dp', 'ctx'), may hold values from -6 to 6
- seq_lengths: int32 [16], P('dp'), may hold values from 1 to 1024, 10240 in all
- tok_perm: int32 [16, 1024], P('dp'), may hold values from 0 to 1023, as said below
- valid_count: int32 [1], replicated, may hold values from 512 to 16384
Outputs:
- activations: bfloat16 [16, 1024, 768], P('dp', 'ctx')
- loss: float32 [1], replicated
- token_grad: float32 [16, 1024, 768], P('dp', 'ctx')
- w_query_grad: float32 [768, 768], P('dp')
- w_key_grad: float32 [768, 768], P('dp')
- w_value_grad: float32 [768, 768], P('dp')
- w_out_grad: float32 [768, 768], P('dp')
- w_up_grad: float32 [768, 3072], P('dp')
- w_down_grad: float32 [3072, 768], P('dp')
- gain_attn_grad: float32 [768], P('dp')
- gain_ffn_grad: float32 [768], P('dp')
Inputs may be any that keep to these rules, and one draw needn't show every extreme that they name: `tok_perm`: each row is a permutation of 0 to 1023. With G = 2 and B = 512 // G, dealt row c * 512 + t * B + j (0 <= j < B) holds a position from t * 512 to (t + 1) * 512 - 1. `seq_lengths`: the longest sequence has exactly 1024 valid tokens; all together have 5 * 1024 * 2.
All inputs are finite; a program needn't handle non-finite values. No bound on the sum of `seq_lengths` on one device may be relied on, other than what follows from the above.
Results may differ from a plain program's by a relative error of at most 0.023.
Values may be sent and summed in bfloat16 or wider, within the bound.
A program may use at most 192 MiB of HBM per device.

v0:
```python
import math

import jax
import jax.numpy as jnp
from jax import lax
from jax.sharding import PartitionSpec as P

HEAD_DIM = 64


EPSILON = 1e-06
SCORE_SCALE = 0.125
MASKED = -1e30


def gelu_exact(values):
    return 0.5 * values * (1.0 + lax.erf(values * 0.7071067811865476))


def norm_forward(hidden, gain_row):
    center = hidden - jnp.mean(hidden, axis=-1, keepdims=True)
    inverse = lax.rsqrt(jnp.mean(center * center, axis=-1, keepdims=True) + EPSILON)
    normal = center * inverse
    return (normal * gain_row, normal, inverse)


def norm_backward(grad_norm, gain_row, normal, inverse):
    scaled = grad_norm * gain_row
    grad_input = inverse * (
        scaled
        - jnp.mean(scaled, axis=-1, keepdims=True)
        - normal * jnp.mean(scaled * normal, axis=-1, keepdims=True)
    )
    return (grad_input, jnp.sum(grad_norm * normal, axis=0))


def row_product(left_mat, right_mat):
    return lax.dot_general(
        left_mat, right_mat, (((0,), (0,)), ((), ())), preferred_element_type=jnp.float32
    )


def by_transpose(left_mat, right_mat):
    return lax.dot_general(
        left_mat, right_mat, (((1,), (1,)), ((), ())), preferred_element_type=jnp.float32
    )


def shards(
    tokens,
    w_query,
    w_key,
    w_value,
    w_out,
    w_up,
    w_down,
    gain_attn,
    gain_ffn,
    teacher,
    seq_lengths,
    tok_perm,
    valid_count,
):
    ctx_count = lax.axis_size("ctx")
    ctx_rank = lax.axis_index("ctx")
    dp_count = lax.axis_size("dp")
    layer_in = tokens[0]
    span_rows, model_width = layer_in.shape
    head_count = model_width // HEAD_DIM
    dealt_order = tok_perm[0]
    seq_len = dealt_order.shape[0]
    length = seq_lengths[0]
    keep_all = dealt_order < length
    per_peer = span_rows // ctx_count
    query_weight, key_weight, value_weight, out_weight, gain_first = (
        lax.all_gather(w_query, "dp", axis=0, tiled=True),
        lax.all_gather(w_key, "dp", axis=0, tiled=True),
        lax.all_gather(w_value, "dp", axis=0, tiled=True),
        lax.all_gather(w_out, "dp", axis=0, tiled=True),
        lax.all_gather(gain_attn, "dp", axis=0, tiled=True),
    )
    up_weight, down_weight, gain_second = (
        lax.all_gather(w_up, "dp", axis=0, tiled=True),
        lax.all_gather(w_down, "dp", axis=0, tiled=True),
        lax.all_gather(gain_ffn, "dp", axis=0, tiled=True),
    )
    queries = jnp.dot(layer_in, query_weight, preferred_element_type=jnp.float32).astype(
        jnp.bfloat16
    )
    keys_own = jnp.dot(layer_in, key_weight, preferred_element_type=jnp.float32).astype(
        jnp.bfloat16
    )
    values_own = jnp.dot(layer_in, value_weight, preferred_element_type=jnp.float32).astype(
        jnp.bfloat16
    )
    query_heads = queries.reshape(span_rows, head_count, HEAD_DIM)
    initial = (
        jnp.full((head_count, span_rows), MASKED, jnp.float32),
        jnp.zeros((head_count, span_rows), jnp.float32),
        jnp.zeros((head_count, span_rows, HEAD_DIM), jnp.float32),
    )
    fold_state = initial
    key_piece = lax.all_gather(keys_own, "ctx", axis=0, tiled=True)
    value_piece = lax.all_gather(values_own, "ctx", axis=0, tiled=True)
    piece_rows = key_piece.shape[0]
    block_rows = math.gcd(piece_rows, span_rows)
    key_blocks = key_piece.reshape(piece_rows // block_rows, block_rows, head_count, HEAD_DIM)
    value_blocks = value_piece.reshape(piece_rows // block_rows, block_rows, head_count, HEAD_DIM)

    def step_block(block_state, block_item):
        running_max, running_sum, accumulated = block_state
        key_block, value_block, block_index = block_item
        key_keep = lax.dynamic_slice_in_dim(keep_all, block_index * block_rows, block_rows)
        scores = (
            jnp.einsum("qhe,khe->hqk", query_heads, key_block, preferred_element_type=jnp.float32)
            * SCORE_SCALE
        )
        scores = jnp.where(key_keep[None, None, :], scores, MASKED)
        new_max = jnp.maximum(running_max, jnp.max(scores, axis=-1))
        factor = jnp.exp(running_max - new_max)
        soft_weights = jnp.where(key_keep[None, None, :], jnp.exp(scores - new_max[..., None]), 0.0)
        running_sum = running_sum * factor + jnp.sum(soft_weights, axis=-1)
        accumulated = accumulated * factor[..., None] + jnp.einsum(
            "hqk,khe->hqe",
            soft_weights.astype(jnp.bfloat16),
            value_block,
            preferred_element_type=jnp.float32,
        )
        return ((new_max, running_sum, accumulated), None)

    block_indices = jnp.arange(piece_rows // block_rows, dtype=jnp.int32)
    fold_state, unused = lax.scan(step_block, fold_state, (key_blocks, value_blocks, block_indices))
    run_max, run_sum, accumulated = fold_state
    log_total = run_max + jnp.log(run_sum)
    attn_full = jnp.transpose(accumulated / run_sum[..., None], (1, 0, 2)).reshape(
        span_rows, model_width
    )
    attn_low = attn_full.astype(jnp.bfloat16)
    gain_first32 = gain_first.astype(jnp.float32)
    gain_second32 = gain_second.astype(jnp.float32)
    branch = jnp.dot(attn_low, out_weight, preferred_element_type=jnp.float32)
    normed, normal_first, inverse_first = norm_forward(
        layer_in.astype(jnp.float32) + branch, gain_first32
    )
    normed_low = normed.astype(jnp.bfloat16)
    upward = jnp.dot(normed_low, up_weight, preferred_element_type=jnp.float32)
    active, gelu_pull = jax.vjp(gelu_exact, upward)
    active_low = active.astype(jnp.bfloat16)
    down_out = jnp.dot(active_low, down_weight, preferred_element_type=jnp.float32)
    result, normal_second, inverse_second = norm_forward(normed + down_out, gain_second32)
    result_low = result.astype(jnp.bfloat16)
    arrived = lax.all_to_all(result_low, "ctx", split_axis=0, concat_axis=0, tiled=True)
    sources = (
        jnp.arange(ctx_count, dtype=jnp.int32)[:, None] * span_rows
        + ctx_rank * per_peer
        + jnp.arange(per_peer, dtype=jnp.int32)[None, :]
    ).reshape(span_rows)
    local_pos = jnp.take(dealt_order, sources) - ctx_rank * span_rows
    in_order = jnp.zeros_like(arrived).at[local_pos].set(arrived)
    target = teacher[0].astype(jnp.float32)
    live_rows = (ctx_rank * span_rows + jnp.arange(span_rows, dtype=jnp.int32) < length)[:, None]
    residual_err = jnp.where(live_rows, in_order.astype(jnp.float32) - target, 0.0)
    total_sq = lax.psum(jnp.sum(residual_err * residual_err), ("dp", "ctx"))
    valid_total = valid_count[0].astype(jnp.float32)
    loss_value = (total_sq / (2.0 * model_width * valid_total)).reshape(1)
    grad_scale = seq_len * dp_count / valid_total
    grad_order = (residual_err * grad_scale).astype(jnp.bfloat16)
    outgoing = jnp.take(grad_order, local_pos, axis=0)
    grad_result = lax.all_to_all(outgoing, "ctx", split_axis=0, concat_axis=0, tiled=True).astype(
        jnp.float32
    )
    grad_sum_second, grad_gain_second = norm_backward(
        grad_result, gain_second32, normal_second, inverse_second
    )
    down_grad_low = grad_sum_second.astype(jnp.bfloat16)
    grad_down_w = row_product(active_low, down_grad_low)
    grad_active = by_transpose(down_grad_low, down_weight)
    grad_upward = gelu_pull(grad_active)[0].astype(jnp.bfloat16)
    grad_up_w = row_product(normed_low, grad_upward)
    grad_normed = grad_sum_second + by_transpose(grad_upward, up_weight)
    grad_hidden, grad_gain_first = norm_backward(
        grad_normed, gain_first32, normal_first, inverse_first
    )
    branch_grad = grad_hidden.astype(jnp.bfloat16)
    grad_out_w = row_product(attn_low, branch_grad)
    attn_grad_low = by_transpose(branch_grad, out_weight).astype(jnp.bfloat16)
    grad_heads = attn_grad_low.reshape(span_rows, head_count, HEAD_DIM)
    row_delta = jnp.sum(
        (attn_grad_low.astype(jnp.float32) * attn_full).reshape(span_rows, head_count, HEAD_DIM),
        axis=-1,
    ).T
    keys_all, values_all = (
        lax.all_gather(keys_own, "ctx", axis=0, tiled=True),
        lax.all_gather(values_own, "ctx", axis=0, tiled=True),
    )
    blocks_count = seq_len // span_rows
    key_stack = keys_all.reshape(blocks_count, span_rows, head_count, HEAD_DIM)
    value_stack = values_all.reshape(blocks_count, span_rows, head_count, HEAD_DIM)

    def score_terms(
        query_block, grad_block, total_block, delta_block, key_block, value_block, key_keep
    ):
        scores = (
            jnp.einsum("qhe,khe->hqk", query_block, key_block, preferred_element_type=jnp.float32)
            * SCORE_SCALE
        )
        soft_weights = jnp.where(
            key_keep[None, None, :], jnp.exp(scores - total_block[..., None]), 0.0
        )
        prob_grad = jnp.einsum(
            "qhe,khe->hqk", grad_block, value_block, preferred_element_type=jnp.float32
        )
        score_grad = (soft_weights * (prob_grad - delta_block[..., None])).astype(jnp.bfloat16)
        return (soft_weights, score_grad)

    def back_block(query_grad, block_item):
        key_block, value_block, block_index = block_item
        key_keep = lax.dynamic_slice_in_dim(keep_all, block_index * span_rows, span_rows)
        soft_weights, score_grad = score_terms(
            query_heads, grad_heads, log_total, row_delta, key_block, value_block, key_keep
        )
        value_grad = jnp.einsum(
            "hqk,qhe->khe",
            soft_weights.astype(jnp.bfloat16),
            grad_heads,
            preferred_element_type=jnp.float32,
        )
        query_grad = query_grad + SCORE_SCALE * jnp.einsum(
            "hqk,khe->qhe", score_grad, key_block, preferred_element_type=jnp.float32
        )
        key_grad = SCORE_SCALE * jnp.einsum(
            "hqk,qhe->khe", score_grad, query_heads, preferred_element_type=jnp.float32
        )
        return (query_grad, (key_grad, value_grad))

    query_grad, (key_grads, value_grads) = lax.scan(
        back_block,
        jnp.zeros((span_rows, head_count, HEAD_DIM), jnp.float32),
        (key_stack, value_stack, jnp.arange(blocks_count, dtype=jnp.int32)),
    )
    key_grad_sum, value_grad_sum = (
        lax.psum_scatter(
            key_grads.reshape(seq_len, model_width).astype(jnp.bfloat16),
            "ctx",
            scatter_dimension=0,
            tiled=True,
        ).astype(jnp.float32),
        lax.psum_scatter(
            value_grads.reshape(seq_len, model_width).astype(jnp.bfloat16),
            "ctx",
            scatter_dimension=0,
            tiled=True,
        ).astype(jnp.float32),
    )
    query_grad_low = query_grad.reshape(span_rows, model_width).astype(jnp.bfloat16)
    key_grad_low = key_grad_sum.astype(jnp.bfloat16)
    value_grad_low = value_grad_sum.astype(jnp.bfloat16)
    grad_query_w = row_product(layer_in, query_grad_low)
    grad_key_w = row_product(layer_in, key_grad_low)
    grad_value_w = row_product(layer_in, value_grad_low)
    token_grad = (
        grad_hidden
        + by_transpose(query_grad_low, query_weight)
        + by_transpose(key_grad_low, key_weight)
        + by_transpose(value_grad_low, value_weight)
    )
    up_part, down_part, second_part = (
        lax.psum_scatter(
            grad_up_w.astype(jnp.bfloat16), "dp", scatter_dimension=0, tiled=True
        ).astype(jnp.float32),
        lax.psum_scatter(
            grad_down_w.astype(jnp.bfloat16), "dp", scatter_dimension=0, tiled=True
        ).astype(jnp.float32),
        lax.psum_scatter(
            grad_gain_second.astype(jnp.bfloat16), "dp", scatter_dimension=0, tiled=True
        ).astype(jnp.float32),
    )
    query_part, key_part, value_part, out_part, first_part = (
        lax.psum_scatter(
            grad_query_w.astype(jnp.bfloat16), "dp", scatter_dimension=0, tiled=True
        ).astype(jnp.float32),
        lax.psum_scatter(
            grad_key_w.astype(jnp.bfloat16), "dp", scatter_dimension=0, tiled=True
        ).astype(jnp.float32),
        lax.psum_scatter(
            grad_value_w.astype(jnp.bfloat16), "dp", scatter_dimension=0, tiled=True
        ).astype(jnp.float32),
        lax.psum_scatter(
            grad_out_w.astype(jnp.bfloat16), "dp", scatter_dimension=0, tiled=True
        ).astype(jnp.float32),
        lax.psum_scatter(
            grad_gain_first.astype(jnp.bfloat16), "dp", scatter_dimension=0, tiled=True
        ).astype(jnp.float32),
    )
    summed = (
        lax.psum(query_part.astype(jnp.bfloat16), "ctx").astype(jnp.float32),
        lax.psum(key_part.astype(jnp.bfloat16), "ctx").astype(jnp.float32),
        lax.psum(value_part.astype(jnp.bfloat16), "ctx").astype(jnp.float32),
        lax.psum(out_part.astype(jnp.bfloat16), "ctx").astype(jnp.float32),
        lax.psum(up_part.astype(jnp.bfloat16), "ctx").astype(jnp.float32),
        lax.psum(down_part.astype(jnp.bfloat16), "ctx").astype(jnp.float32),
        lax.psum(first_part.astype(jnp.bfloat16), "ctx").astype(jnp.float32),
        lax.psum(second_part.astype(jnp.bfloat16), "ctx").astype(jnp.float32),
    )
    query_sum, key_sum, value_sum, out_sum, up_sum, down_sum, first_sum, second_sum = summed
    return (
        in_order[None],
        loss_value,
        token_grad[None],
        query_sum,
        key_sum,
        value_sum,
        out_sum,
        up_sum,
        down_sum,
        first_sum,
        second_sum,
    )


def solution(mesh):
    in_specs = (
        P("dp", "ctx", None),
        P("dp", None),
        P("dp", None),
        P("dp", None),
        P("dp", None),
        P("dp", None),
        P("dp", None),
        P("dp"),
        P("dp"),
        P("dp", "ctx", None),
        P("dp"),
        P("dp", None),
        P(),
    )
    out_specs = (
        P("dp", "ctx", None),
        P(),
        P("dp", "ctx", None),
        P("dp", None),
        P("dp", None),
        P("dp", None),
        P("dp", None),
        P("dp", None),
        P("dp", None),
        P("dp"),
        P("dp"),
    )
    return jax.shard_map(shards, mesh=mesh, in_specs=in_specs, out_specs=out_specs, check_vma=False)
```

profile of v0, /device:TPU:0, one launch (start us, length us, event | category | flops | bytes accessed | tf_op | source)
XLA Modules:
  0.0 985.0 jit_solution(12747516293233823391)
XLA Ops:
  9.5 41.9 %all-gather.9.cloned.1.call-done = bf16[768,768]{1,0:T(8,128)(2,1)} async-done(((bf16[48,768]{1,0:T(8,128)(2,1)}), bf16[768,768]{1,0:T(8,128)(2,1)}) %all-gather.9.cloned.1.call-update) | async-done | bytes 1179664 | tf_op jit(solution)/shard_map/all_gather | solution.py:77
  51.4 3.2 convolution_convert_fusion.9
  54.7 36.3 %all-gather.15.cloned.1.call-done = bf16[768,768]{1,0:T(8,128)(2,1)} async-done(((bf16[48,768]{1,0:T(8,128)(2,1)}), bf16[768,768]{1,0:T(8,128)(2,1)}) %all-gather.15.cloned.1.call-update) | async-done | bytes 1179664 | tf_op jit(solution)/shard_map/all_gather | solution.py:78
  91.0 2.9 convolution_convert_fusion.7
  98.6 32.0 %all-reduce.5 = (bf16[768]{0:T(1024)(128)(2,1)S(1)}, bf16[768]{0:T(1024)(128)(2,1)S(1)}) all-reduce(bf16[768]{0:T(1024)(128)(2,1)S(1)} %dynamic-update-slice, bf16[768]{0:T(1024)(128)(2,1)S(1)} %dynamic-update-slice.1), channel_id=1, replica_groups=mesh['dp'=16,'ctx'=2] {'dp'}, use_global_device_ids=true, to_apply=%add | all-reduce | flops 1536 | bytes 6144
  135.9 23.0 %all-gather.11.cloned.1.call-done = bf16[1024,768]{1,0:T(8,128)(2,1)} async-done(((bf16[512,768]{1,0:T(8,128)(2,1)}), bf16[1024,768]{1,0:T(8,128)(2,1)}) %all-gather.11.cloned.1.call-update) | async-done | bytes 1572880 | tf_op jit(solution)/shard_map/all_gather | solution.py:103
  161.5 3.8 reshape.229
  165.4 3.1 copy.56
  168.4 19.1 %all-gather.17.cloned.1.call-done = bf16[1024,768]{1,0:T(8,128)(2,1)} async-done(((bf16[512,768]{1,0:T(8,128)(2,1)}), bf16[1024,768]{1,0:T(8,128)(2,1)}) %all-gather.17.cloned.1.call-update) | async-done | bytes 1572880 | tf_op jit(solution)/shard_map/all_gather | solution.py:104
  187.6 2.7 copy.55
  190.2 3.9 reshape.231
  194.1 2.9 copy.57
  197.0 47.9 %while.30 = (s32[]{:T(128)}, f32[12,512]{1,0:T(8,128)S(1)}, f32[12,512]{1,0:T(8,128)S(1)}, f32[12,512,64]{1,2,0:T(8,128)}, s32[2]{0:T(128)S(1)}, /*index=5*/pred...) while((s32[]{:T(128)}, f32[12,512]{1,0:T(8,128)S(1)}, ...), condition=%wide.region_3.4_spmd.clone, body=%wide.region_0.3_spmd.clone.sunk | while | flops 847411200 | bytes 93999328 | solution.py:132
  198.3 8.5 bitcast_reduce_fusion.2
  206.8 7.1 fusion.125
  215.2 5.4 fusion.127
  221.9 8.5 bitcast_reduce_fusion.2
  230.4 7.1 fusion.125
  239.0 5.9 fusion.127
  244.9 2.8 broadcast_divide_fusion
  251.9 30.8 %all-gather.21.cloned.1.call-done = bf16[768,3072]{1,0:T(8,128)(2,1)} async-done(((bf16[48,3072]{1,0:T(8,128)(2,1)}), bf16[768,3072]{1,0:T(8,128)(2,1)}) %all-gather.21.cloned.1.call-update) | async-done | bytes 4718608 | tf_op jit(solution)/shard_map/all_gather | solution.py:83
  282.7 8.6 multiply_convert_fusion.1
  291.4 45.6 %all-gather.23.cloned.1.call-done = bf16[3072,768]{1,0:T(8,128)(2,1)} async-done(((bf16[192,768]{1,0:T(8,128)(2,1)}), bf16[3072,768]{1,0:T(8,128)(2,1)}) %all-gather.23.cloned.1.call-update) | async-done | bytes 4718608 | tf_op jit(solution)/shard_map/all_gather | solution.py:84
  337.0 6.4 fusion.73
  344.9 3.5 all-to-all-start
  348.5 11.4 %all-to-all-done = bf16[2,256,768]{2,1,0:T(8,128)(2,1)S(1)} async-done(((bf16[2,256,768]{2,1,0:T(8,128)(2,1)}), bf16[2,256,768]{2,1,0:T(8,128)(2,1)S(1)}, u32[]{:S(2)}, u32[]{:S(2)}) %all-to-all-start) | async-done | bytes 786464 | tf_op jit(solution)/shard_map/all_to_all | solution.py:152
  359.9 2.9 scatter_custom_fusion
  362.8 2.7 multiply_convert_fusion.2
  365.5 2.7 gather_fusion.1
  370.4 3.5 all-to-all-start.1
  374.0 3.1 copy.59
  377.1 7.5 all-to-all-done.1
  384.6 2.8 fusion.47
  388.2 8.1 add_convert_fusion
  396.4 3.1 multiply_reduce_fusion
  403.2 3.0 copy.60
  408.1 55.9 %while.31 = (s32[]{:T(128)}, f32[512,12,64]{0,2,1:T(8,128)}, bf16[2,512,12,64]{1,3,2,0:T(8,128)(2,1)}, bf16[2,512,12,64]{1,3,2,0:T(8,128)(2,1)}, bf16[2,512,12,6...) while((s32[]{:T(128)}, f32[512,12,64]{0,2,1:T(8,128)}, ...), condition=%wide.region_17.18_spmd.clone, body=%wide.region_16.17_spmd.clone.sunk | while | flops 2046296064 | bytes 200634704 | solution.py:236
  409.6 3.1 fusion.138
  412.7 4.5 copy-done.3
  417.3 6.0 multiply_convert_fusion.8
  423.2 5.4 bitcast_add_fusion.2
  428.7 2.9 bitcast_dynamic-update-slice_fusion.4
  432.5 3.4 bitcast_dynamic-update-slice_fusion.5
  437.2 3.1 fusion.138
  440.3 4.5 copy-done.3
  444.8 6.0 multiply_convert_fusion.8
  450.8 5.9 bitcast_add_fusion.2
  456.7 2.9 bitcast_dynamic-update-slice_fusion.4
  460.6 3.4 bitcast_dynamic-update-slice_fusion.5
  464.0 3.0 copy.63
  478.2 14.3 %reduce-scatter.15.cloned.1.call-done = bf16[512,768]{0,1:T(8,128)(2,1)} async-done(((bf16[1024,768]{0,1:T(8,128)(2,1)}), bf16[512,768]{0,1:T(8,128)(2,1)}) %reduce-scatter.15.cloned.1.call-update) | async-done | bytes 786448 | tf_op jit(solution)/shard_map/reduce_scatter | solution.py:242
  495.9 24.8 %reduce-scatter.17.cloned.1.call-done = bf16[512,768]{0,1:T(8,128)(2,1)} async-done(((bf16[1024,768]{0,1:T(8,128)(2,1)}), bf16[512,768]{0,1:T(8,128)(2,1)}) %reduce-scatter.17.cloned.1.call-update) | async-done | bytes 786448 | tf_op jit(solution)/shard_map/reduce_scatter | solution.py:248
  520.8 3.0 fusion.50
  528.2 7.4 convolution_convert_fusion.1
  537.0 6.8 convolution_convert_fusion
  544.6 39.7 %psum.63 = f32[]{:T(128)} all-reduce(f32[]{:T(128)} %get-tuple-element.359), channel_id=1, replica_groups=mesh['dp'=16,'ctx'=2] {'dp','ctx'}, use_global_device_ids=true, to_apply=%region_10.11 | all-reduce | flops 1 | bytes 8 | tf_op jit(solution)/shard_map/psum | solution.py:163
  586.6 56.4 %reduce-scatter.27.cloned.1.call-done = bf16[48,768]{1,0:T(8,128)(2,1)} async-done(((bf16[768,768]{1,0:T(8,128)(2,1)}), bf16[48,768]{1,0:T(8,128)(2,1)}) %reduce-scatter.27.cloned.1.call-update) | async-done | bytes 73744
  644.7 59.1 %reduce-scatter.29.cloned.1.call-done = bf16[48,768]{1,0:T(8,128)(2,1)} async-done(((bf16[768,768]{1,0:T(8,128)(2,1)}), bf16[48,768]{1,0:T(8,128)(2,1)}) %reduce-scatter.29.cloned.1.call-update) | async-done | bytes 73744
  705.5 59.5 %reduce-scatter.19.cloned.1.call-done = bf16[48,768]{1,0:T(8,128)(2,1)} async-done(((bf16[768,768]{1,0:T(8,128)(2,1)}), bf16[48,768]{1,0:T(8,128)(2,1)}) %reduce-scatter.19.cloned.1.call-update) | async-done | bytes 73744 | tf_op jit(solution)/shard_map/reduce_scatter | solution.py:288
  764.9 78.3 %reduce-scatter.21.cloned.1.call-done = bf16[48,3072]{1,0:T(8,128)(2,1)} async-done(((bf16[768,3072]{1,0:T(8,128)(2,1)}), bf16[48,3072]{1,0:T(8,128)(2,1)}) %reduce-scatter.21.cloned.1.call-update) | async-done | bytes 294928 | tf_op jit(solution)/shard_map/reduce_scatter | solution.py:268
  843.2 78.9 %reduce-scatter.23.cloned.1.call-done = bf16[192,768]{1,0:T(8,128)(2,1)} async-done(((bf16[3072,768]{1,0:T(8,128)(2,1)}), bf16[192,768]{1,0:T(8,128)(2,1)}) %reduce-scatter.23.cloned.1.call-update) | async-done | bytes 294928 | tf_op jit(solution)/shard_map/reduce_scatter | solution.py:271
  924.5 30.0 %all-reduce.4 = (bf16[768]{0:T(1024)(128)(2,1)S(1)}, bf16[768]{0:T(1024)(128)(2,1)S(1)}) all-reduce(bf16[768]{0:T(1024)(128)(2,1)S(1)} %get-tuple-element.295, bf16[768]{0:T(1024)(128)(2,1)S(1)} %copy-done.29), channel_id=10, replica_groups=mesh['dp'=16,'ctx'=2] {'dp'}, use_global_device_ids=true, to_apply=%region_33.34.clone | all-reduce | flops 1536 | bytes 6144
  954.7 5.0 all-reduce.6
  965.2 5.2 all-reduce.10.cloned.1.call-done
  (208 shorter events, 74.7 us)
Async XLA Ops:
  7.2 44.2 %all-gather.9.cloned.1.call-start = ((), (), s32[]{:S(2)}) async-start(), calls=%async_computation.10 | async-start | bytes 1253376 | tf_op jit(solution)/shard_map/all_gather | solution.py:77
  7.9 83.0 %all-gather.15.cloned.1.call-start = ((), (), s32[]{:S(2)}) async-start(), calls=%async_computation.13 | async-start | bytes 1253376 | tf_op jit(solution)/shard_map/all_gather | solution.py:78
  8.7 124.9 %all-gather.13.cloned.1.call-start = ((), (), s32[]{:S(2)}) async-start(), calls=%async_computation.12 | async-start | bytes 1253376 | tf_op jit(solution)/shard_map/all_gather | solution.py:76
  9.4 81.6 %copy-start.21 = (bf16[1,512,768]{2,1,0:T(8,128)(2,1)S(1)}, bf16[1,512,768]{2,1,0:T(8,128)(2,1)}, u32[]{:S(2)}) copy-start(bf16[1,512,768]{2,1,0:T(8,128)(2,1)} %param.17) | copy-start | bytes 2359300
  9.4 149.5 %all-gather.11.cloned.1.call-start = ((), (), s32[]{:S(2)}) async-start(), calls=%async_computation.11 | async-start | bytes 2359296 | tf_op jit(solution)/shard_map/all_gather | solution.py:103
  54.6 42.2 %copy-start.1 = (s32[1,1024]{1,0:T(1,128)S(1)}, s32[1,1024]{1,0:T(1,128)}, u32[]{:S(2)}) copy-start(s32[1,1024]{1,0:T(1,128)} %param.28) | copy-start | bytes 12292
  54.6 42.2 %copy-start.30 = (u32[32]{0:T(128)S(1)}, u32[32]{0:T(128)}, u32[]{:S(2)}) copy-start(u32[32]{0:T(128)} %constant.127) | copy-start | bytes 388
  54.6 43.5 %copy-start.31 = (bf16[48]{0:T(256)(128)(2,1)S(1)}, bf16[48]{0:T(256)(128)(2,1)}, u32[]{:S(2)}) copy-start(bf16[48]{0:T(256)(128)(2,1)} %param.24) | copy-start | bytes 292
  54.6 43.7 %copy-start.32 = (bf16[48]{0:T(256)(128)(2,1)S(1)}, bf16[48]{0:T(256)(128)(2,1)}, u32[]{:S(2)}) copy-start(bf16[48]{0:T(256)(128)(2,1)} %param.25) | copy-start | bytes 292
  54.6 133.0 %all-gather.17.cloned.1.call-start = ((), (), s32[]{:S(2)}) async-start(), calls=%async_computation.14 | async-start | bytes 2359296 | tf_op jit(solution)/shard_map/all_gather | solution.py:104
  93.9 153.8 %all-gather.19.cloned.1.call-start = ((), (), s32[]{:S(2)}) async-start(), calls=%async_computation.15 | async-start | bytes 1253376 | tf_op jit(solution)/shard_map/all_gather | solution.py:79
  94.5 188.2 %all-gather.21.cloned.1.call-start = ((), (), s32[]{:S(2)}) async-start(), calls=%async_computation.16 | async-start | bytes 5013504 | tf_op jit(solution)/shard_map/all_gather | solution.py:83
  95.2 241.7 %all-gather.23.cloned.1.call-start = ((), (), s32[]{:S(2)}) async-start(), calls=%async_computation.17 | async-start | bytes 5013504 | tf_op jit(solution)/shard_map/all_gather | solution.py:84
  206.8 8.4 copy-start
  230.4 8.5 copy-start
  250.4 1.2 copy-start.11
  343.4 1.5 copy-start.7
  344.9 15.0 %all-to-all-start = ((bf16[2,256,768]{2,1,0:T(8,128)(2,1)}), bf16[2,256,768]{2,1,0:T(8,128)(2,1)S(1)}, u32[]{:S(2)}, u32[]{:S(2)}) async-start(bf16[2,256,768]{2,1,0:T(8,128)(2,1)} %bitcast.10), calls=%async_computation | async-start | bytes 1572864 | tf_op jit(solution)/shard_map/all_to_all | solution.py:152
  362.8 5.4 copy-start.15
  370.4 14.2 %all-to-all-start.1 = ((bf16[2,256,768]{2,1,0:T(8,128)(2,1)}), bf16[2,256,768]{2,1,0:T(8,128)(2,1)S(1)}, u32[]{:S(2)}, u32[]{:S(2)}) async-start(bf16[2,256,768]{2,1,0:T(8,128)(2,1)} %broadcast_select_fusion), calls=%async_computation.1 | async-start | bytes 1572864 | tf_op jit(solution)/shard_map/all_to_all | solution.py:169
  373.9 118.5 %reduce-scatter.15.cloned.1.call-start = ((), (), s32[]{:S(2)}) async-start(), calls=%async_computation.18 | async-start | bytes 2359296 | tf_op jit(solution)/shard_map/reduce_scatter | solution.py:242
  384.6 3.0 copy-start.8
  387.6 8.7 slice-start
  388.1 8.2 copy-start.17
  388.1 8.2 copy-start.12
  388.1 8.2 slice-start.1
  396.3 3.1 copy-start.33
  399.4 1.4 copy-start.13
  399.4 1.7 copy-start.14
  401.2 2.0 copy-start.9
  409.6 7.6 copy-start.16
  412.7 4.5 copy-start.3
  423.2 5.5 copy-start.2
  423.2 9.3 copy-start.4
  437.2 7.6 copy-start.16
  440.3 4.5 copy-start.3
  450.8 5.9 copy-start.2
  450.8 9.7 copy-start.4
  468.6 1.4 copy-start.19
  468.6 52.2 %reduce-scatter.17.cloned.1.call-start = ((), (), s32[]{:S(2)}) async-start(), calls=%async_computation.19 | async-start | bytes 2359296 | tf_op jit(solution)/shard_map/reduce_scatter | solution.py:248
  473.3 1.4 copy-start.5
  473.3 2.4 copy-start.22
  473.3 111.6 %reduce-scatter.25.cloned.1.call-start = ((), (), s32[]{:S(2)}) async-start(), calls=%async_computation.23 | async-start | bytes 1253376
  474.8 0.9 copy-start.23
  477.9 165.1 %reduce-scatter.27.cloned.1.call-start = ((), (), s32[]{:S(2)}) async-start(), calls=%async_computation.24 | async-start | bytes 1253376
  495.9 207.9 %reduce-scatter.29.cloned.1.call-start = ((), (), s32[]{:S(2)}) async-start(), calls=%async_computation.25 | async-start | bytes 1253376
  523.7 2.6 copy-start.6
  523.7 2.6 copy-start.10
  526.3 238.6 %reduce-scatter.19.cloned.1.call-start = ((), (), s32[]{:S(2)}) async-start(), calls=%async_computation.20 | async-start | bytes 1253376 | tf_op jit(solution)/shard_map/reduce_scatter | solution.py:288
  528.2 315.0 %reduce-scatter.21.cloned.1.call-start = ((), (), s32[]{:S(2)}) async-start(), calls=%async_computation.21 | async-start | bytes 5013504 | tf_op jit(solution)/shard_map/reduce_scatter | solution.py:268
  535.6 1.4 copy-start.18
  535.6 386.5 %reduce-scatter.23.cloned.1.call-start = ((), (), s32[]{:S(2)}) async-start(), calls=%async_computation.22 | async-start | bytes 5013504 | tf_op jit(solution)/shard_map/reduce_scatter | solution.py:271
  543.9 426.5 %all-reduce.10.cloned.1.call-start = ((), (), s32[]{:S(2)}) async-start(), calls=%async_computation.26 | async-start | bytes 2506752 | tf_op jit(solution)/shard_map/psum | solution.py:296
  922.1 2.4 copy-start.29
  960.7 2.5 copy-start.20
  960.7 2.5 copy-start.24
  970.4 3.7 copy-start.28
  970.4 4.4 copy-start.27
  970.4 5.2 copy-start.26
  970.4 6.0 copy-start.25
Sparse Core Ops, SparseCore 0:
  10.3 41.0 all-gather.8
  53.6 37.2 all-gather.14
  93.2 37.4 all-gather.12
  132.7 26.1 all-gather.10
  160.3 27.2 all-gather.16
  189.7 38.3 all-gather.18
  230.3 52.3 all-gather.20
  285.0 51.9 all-gather.22
  468.7 23.6 reduce-scatter.14
  494.6 26.0 reduce-scatter.16
  524.4 58.0 reduce-scatter.24
  586.0 56.9 reduce-scatter.26
  646.6 57.1 reduce-scatter.28
  707.8 57.0 reduce-scatter.18
  768.6 74.5 reduce-scatter.20
  847.4 74.6 reduce-scatter.22
  925.7 44.5 all-reduce.9
where the time goes:
time: 989 us; the launch traced here: 985 us
  waiting for transfers between devices  596 us (60%)
  matrix products  138 us (14%)
  blocking collectives  107 us (11%)
  local copies, waits for them, and re-layouts  79.1 us (8%)
  other arithmetic  35 us (4%)
  between operations  19.2 us (2%)
    unnamed x20, waiting for transfers between devices  120 us
    reduce_scatter x1, waiting for transfers between devices, shards(): lax.psum_scatter(grad_down_w.astype(jnp.bfloat16), 'dp', scatter_dimensio...  78.9 us
    reduce_scatter x1, waiting for transfers between devices, shards(): lax.psum_scatter(grad_up_w.astype(jnp.bfloat16), 'dp', scatter_dimension=...  78.3 us
    unnamed x2, blocking collectives  62 us
    reduce_scatter x1, waiting for transfers between devices, shards(): lax.psum_scatter(grad_out_w.astype(jnp.bfloat16), 'dp', scatter_dimension...  59.5 us
    all_gather x1, waiting for transfers between devices, shards(): lax.all_gather(w_down, 'dp', axis=0, tiled=True)  45.6 us
    all_gather x1, waiting for transfers between devices, shards(): lax.all_gather(w_key, 'dp', axis=0, tiled=True)  41.9 us
    psum x1, blocking collectives, shards(): total_sq = lax.psum(jnp.sum(residual_err * residual_err), ('dp', 'ctx'))  39.7 us
  transfers between devices with their start and end apart: 19, of which 16 were waited for; matrix products, arithmetic and copies ran while one was open for 14% of the time, Pallas kernels for 0%

commit v1 on v0

--- a/solution.py
+++ b/solution.py
@@ -1,8 +1,11 @@
+import functools
 import math
 
 import jax
 import jax.numpy as jnp
 from jax import lax
+from jax.experimental import pallas as pl
+from jax.experimental.pallas import tpu as pltpu
 from jax.sharding import PartitionSpec as P
 
 HEAD_DIM = 64
@@ -11,6 +14,8 @@
 EPSILON = 1e-06
 SCORE_SCALE = 0.125
 MASKED = -1e30
+MESH = pl.DeviceIdType.MESH
+MIB = 1024 * 1024
 
 
 def gelu_exact(values):
@@ -318,6 +323,598 @@
     )
 
 
+class Chunk:
+    def __init__(self, rows, cols, first):
+        self.rows, self.cols, self.half = rows, cols, cols // 2
+        self.first, self.second = first, cols // 2 - first
+
+
+class Place:
+    def __init__(self):
+        dp = lax.axis_index("dp")
+        self.x = lax.axis_index("ctx")
+        self.z, self.y, self.c = dp // 4, (dp // 2) % 2, dp % 2
+        self.xo, self.yo, self.co = 1 - self.x, 1 - self.y, 1 - self.c
+        self.to_x = (dp, self.xo)
+        self.to_y = (self.z * 4 + self.yo * 2 + self.c, self.x)
+        self.to_c = (self.z * 4 + self.y * 2 + self.co, self.x)
+        self.z_up = [(self.z + k) % 4 for k in range(4)]
+        self.z_down = [(self.z + 4 - k) % 4 for k in range(4)]
+        self.to_z = [(self.z_up[k] * 4 + self.y * 2 + self.c, self.x) for k in range(4)]
+
+    def partners(self):
+        return [self.to_x, self.to_y, self.to_c] + self.to_z[1:]
+
+    def barrier(self):
+        semaphore = pltpu.get_barrier_semaphore()
+        for partner in self.partners():
+            pl.semaphore_signal(semaphore, inc=1, device_id=partner, device_id_type=MESH)
+        pl.semaphore_wait(semaphore, 6)
+
+
+class Links:
+    def __init__(self, send, recv):
+        self.send, self.recv, self.used, self.all = send, recv, 0, []
+
+    def start(self, src, dst, partner):
+        at = self.used
+        self.used += 1
+        copy = pltpu.make_async_remote_copy(
+            src_ref=src,
+            dst_ref=dst,
+            send_sem=self.send.at[at],
+            recv_sem=self.recv.at[at],
+            device_id=partner,
+            device_id_type=MESH,
+        )
+        copy.start()
+        self.all.append(copy)
+        return copy
+
+    def drain(self):
+        for copy in self.all:
+            copy.wait_send()
+
+
+def columns(start, size):
+    return pl.ds(pl.multiple_of(start, 128), size)
+
+
+class Gather:
+    def __init__(self, chunk, shard, whole, place, links, own_sem):
+        self.chunk, self.shard, self.whole = chunk, shard, whole
+        self.p, self.links = place, links
+        self.own = pltpu.make_async_copy(shard, whole.at[place.z, place.y, place.c], own_sem)
+
+    def half(self, x):
+        return columns(x * self.chunk.half, self.chunk.half)
+
+    def first(self, x):
+        return columns(x * self.chunk.half, self.chunk.first)
+
+    def second(self, x):
+        return columns(x * self.chunk.half + self.chunk.first, self.chunk.second)
+
+    def step0(self):
+        p, whole, shard = self.p, self.whole, self.shard
+        mine = self.half(p.x)
+        self.own.start()
+        self.from_z = [
+            self.links.start(
+                shard.at[:, mine], whole.at[p.z, p.y, p.c, :, mine], p.to_z[k]
+            )
+            for k in range(1, 4)
+        ]
+        self.y_own = self.links.start(
+            shard.at[:, mine], whole.at[p.z, p.y, p.c, :, mine], p.to_y
+        )
+        self.from_c = [self.links.start(shard, whole.at[p.z, p.y, p.c], p.to_c)]
+
+    def step1(self):
+        p, whole = self.p, self.whole
+        mine = self.half(p.x)
+        self.from_x, self.from_y = [], [self.y_own]
+        for k in range(1, 4):
+            self.from_z[k - 1].wait_recv()
+            piece = whole.at[p.z_down[k], p.y, p.c, :, mine]
+            self.from_x.append(self.links.start(piece, piece, p.to_x))
+            self.from_y.append(self.links.start(piece, piece, p.to_y))
+            self.from_c.append(self.links.start(piece, piece, p.to_c))
+
+    def step2(self):
+        p, whole = self.p, self.whole
+        other = self.half(p.xo)
+        self.own.wait()
+        for k in range(1, 4):
+            self.from_x[k - 1].wait_recv()
+            piece = whole.at[p.z_down[k], p.y, p.c, :, other]
+            self.from_c.append(self.links.start(piece, piece, p.to_c))
+        piece = whole.at[:, p.y, p.c, :, self.first(p.xo)]
+        self.first_y = self.links.start(piece, piece, p.to_y)
+        for copy in self.from_y:
+            copy.wait_recv()
+        piece = whole.at[:, p.yo, p.c, :, self.second(p.x)]
+        self.second_x = self.links.start(piece, piece, p.to_x)
+        piece = whole.at[:, p.yo, p.c, :, self.half(p.x)]
+        self.from_c.append(self.links.start(piece, piece, p.to_c))
+
+    def step3(self):
+        p, whole = self.p, self.whole
+        self.first_y.wait_recv()
+        piece = whole.at[:, p.yo, p.c, :, self.first(p.xo)]
+        self.from_c.append(self.links.start(piece, piece, p.to_c))
+        self.second_x.wait_recv()
+        piece = whole.at[:, p.yo, p.c, :, self.second(p.xo)]
+        self.from_c.append(self.links.start(piece, piece, p.to_c))
+
+    def step4(self):
+        for copy in self.from_c:
+            copy.wait_recv()
+
+
+GATHER_COPIES = 23
+
+
+def reduce_scratch(chunk):
+    rows, bf16 = chunk.rows, jnp.bfloat16
+    return [
+        pltpu.VMEM((4, 2, rows, chunk.cols), bf16),
+        pltpu.VMEM((4, 2, rows, chunk.second), bf16),
+        pltpu.VMEM((2, 4, rows, chunk.first), bf16),
+        pltpu.VMEM((4, rows, chunk.second), bf16),
+        pltpu.VMEM((4, rows, chunk.first), bf16),
+        pltpu.VMEM((3, rows, chunk.half), bf16),
+    ]
+
+
+REDUCE_COPIES = 10
+
+
+class Reduce(Gather):
+    def __init__(self, chunk, grads, out, place, links, scratch):
+        self.chunk, self.grads, self.out = chunk, grads, out
+        self.p, self.links = place, links
+        self.core_in, self.x_in, self.y_in, self.y_in2, self.x_in2, self.z_in = scratch
+
+    def add(self, outer, at, source):
+        steps = self.chunk.rows // 16
+
+        def body(i, carry):
+            rows = pl.ds(pl.multiple_of((i % steps) * 16, 16), 16)
+            target = at(i // steps, rows)
+            given = source(i // steps, rows)
+            self.grads[target] = (
+                self.grads[target].astype(jnp.float32) + given.astype(jnp.float32)
+            ).astype(jnp.bfloat16)
+            return carry
+
+        lax.fori_loop(0, outer * steps, body, 0)
+
+    def step0(self):
+        p = self.p
+        self.by_core = self.links.start(self.grads.at[:, :, p.co], self.core_in, p.to_c)
+
+    def step1(self):
+        p, grads = self.p, self.grads
+        self.by_core.wait_recv()
+        everything = pl.ds(0, self.chunk.cols)
+        self.add(
+            8,
+            lambda i, rows: (i // 2, i % 2, p.c, rows, everything),
+            lambda i, rows: self.core_in[i // 2, i % 2, rows, :],
+        )
+        self.by_x = self.links.start(grads.at[:, :, p.c, :, self.second(p.xo)], self.x_in, p.to_x)
+        self.by_y = [
+            self.links.start(grads.at[:, p.yo, p.c, :, self.first(h)], self.y_in.at[h], p.to_y)
+            for h in range(2)
+        ]
+
+    def step2(self):
+        p, grads = self.p, self.grads
+        for h in range(2):
+            self.by_y[h].wait_recv()
+            cut = self.first(h)
+            self.add(
+                4,
+                lambda i, rows: (i, p.y, p.c, rows, cut),
+                lambda i, rows: self.y_in[h, i, rows, :],
+            )
+        self.by_x2 = self.links.start(grads.at[:, p.y, p.c, :, self.first(p.xo)], self.x_in2, p.to_x)
+        self.by_x.wait_recv()
+        cut2 = self.second(p.x)
+        self.add(
+            8,
+            lambda i, rows: (i // 2, i % 2, p.c, rows, cut2),
+            lambda i, rows: self.x_in[i // 2, i % 2, rows, :],
+        )
+        self.by_y2 = self.links.start(grads.at[:, p.yo, p.c, :, cut2], self.y_in2, p.to_y)
+
+    def step3(self):
+        p, grads = self.p, self.grads
+        self.by_x2.wait_recv()
+        cut = self.first(p.x)
+        self.add(
+            4, lambda i, rows: (i, p.y, p.c, rows, cut), lambda i, rows: self.x_in2[i, rows, :]
+        )
+        self.by_y2.wait_recv()
+        cut2 = self.second(p.x)
+        self.add(
+            4, lambda i, rows: (i, p.y, p.c, rows, cut2), lambda i, rows: self.y_in2[i, rows, :]
+        )
+        mine = self.half(p.x)
+        self.by_z = [
+            self.links.start(grads.at[p.z_up[k], p.y, p.c, :, mine], self.z_in.at[k - 1], p.to_z[k])
+            for k in range(1, 4)
+        ]
+
+    def step4(self):
+        p = self.p
+        mine = self.half(p.x)
+        for copy in self.by_z:
+            copy.wait_recv()
+
+        def body(i, carry):
+            rows = pl.ds(pl.multiple_of(i * 16, 16), 16)
+            total = self.grads[p.z, p.y, p.c, rows, mine].astype(jnp.float32)
+            for k in range(3):
+                total = total + self.z_in[k, rows, :].astype(jnp.float32)
+            self.out[rows, mine] = total.astype(jnp.bfloat16)
+            return carry
+
+        lax.fori_loop(0, self.chunk.rows // 16, body, 0)
+        self.last = self.links.start(self.out.at[:, mine], self.out.at[:, mine], p.to_x)
+
+    def step5(self):
+        self.last.wait_recv()
+
+
+class Total:
+    def __init__(self, value, core_in, x_in, y_in, by_z, place, links):
+        self.value, self.core_in, self.x_in, self.y_in, self.by_z = value, core_in, x_in, y_in, by_z
+        self.p, self.links = place, links
+
+    def step0(self):
+        self.copy = self.links.start(self.value.at[0], self.core_in, self.p.to_c)
+
+    def step1(self):
+        self.copy.wait_recv()
+        self.value[1] = self.value[0] + self.core_in[...]
+        self.copy = self.links.start(self.value.at[1], self.x_in, self.p.to_x)
+
+    def step2(self):
+        self.copy.wait_recv()
+        self.value[2] = self.value[1] + self.x_in[...]
+        self.copy = self.links.start(self.value.at[2], self.y_in, self.p.to_y)
+
+    def step3(self):
+        self.copy.wait_recv()
+        z = self.p.z
+        self.by_z[z] = self.value[2] + self.y_in[...]
+        self.copies = [
+            self.links.start(self.by_z.at[z], self.by_z.at[z], self.p.to_z[k]) for k in range(1, 4)
+        ]
+
+    def step4(self):
+        for copy in self.copies:
+            copy.wait_recv()
+        return ((self.by_z[0] + self.by_z[1]) + self.by_z[2]) + self.by_z[3]
+
+
+TOTAL_COPIES = 6
+
+
+def gather_kernel(chunks, *refs):
+    n = len(chunks)
+    shards, tokens, teach = refs[:n], refs[n], refs[n + 1]
+    wholes, tokens_all, teach_in = refs[n + 2 : 2 * n + 2], refs[2 * n + 2], refs[2 * n + 3]
+    send, recv, own_sem = refs[2 * n + 4 :]
+    place = Place()
+    links = Links(send, recv)
+    place.barrier()
+    work = [
+        Gather(chunk, shards[i], wholes[i], place, links, own_sem.at[i])
+        for i, chunk in enumerate(chunks)
+    ]
+    own_tokens = pltpu.make_async_copy(tokens, tokens_all.at[place.x], own_sem.at[n])
+    own_tokens.start()
+    swap = []
+    for item in work:
+        item.step0()
+    swap.append(links.start(tokens, tokens_all.at[place.x], place.to_x))
+    swap.append(links.start(teach, teach_in, place.to_x))
+    for s in range(n + 3):
+        for i, item in enumerate(work):
+            if s - i == 0:
+                item.step1()
+            if s - i == 1:
+                item.step2()
+            if s - i == 2:
+                item.step3()
+            if s - i == 3:
+                item.step4()
+    for copy in swap:
+        copy.wait_recv()
+    own_tokens.wait()
+    links.drain()
+
+
+def gather_all(chunks, shards, tokens, teach):
+    bf16 = jnp.bfloat16
+    n = len(chunks)
+    out_shape = [jax.ShapeDtypeStruct((4, 2, 2, c.rows, c.cols), bf16) for c in chunks]
+    out_shape += [
+        jax.ShapeDtypeStruct((2,) + tokens.shape, bf16),
+        jax.ShapeDtypeStruct(teach.shape, bf16),
+    ]
+    copies = GATHER_COPIES * n + 2
+    return pl.pallas_call(
+        functools.partial(gather_kernel, chunks),
+        out_shape=out_shape,
+        in_specs=[pl.BlockSpec(memory_space=pl.ANY)] * (n + 2),
+        out_specs=[pl.BlockSpec(memory_space=pl.ANY)] * (n + 2),
+        scratch_shapes=[
+            pltpu.SemaphoreType.DMA((copies,)),
+            pltpu.SemaphoreType.DMA((copies,)),
+            pltpu.SemaphoreType.DMA((n + 1,)),
+        ],
+        compiler_params=pltpu.CompilerParams(collective_id=0, has_side_effects=True),
+    )(*shards, tokens, teach)
+
+
+def reduce_kernel(chunks, *refs):
+    n = len(chunks)
+    grads, error, result = refs[:n], refs[n], refs[n + 1]
+    outs, total_out, result_in = refs[n + 2 : 2 * n + 2], refs[2 * n + 2], refs[2 * n + 3]
+    rest = refs[2 * n + 4 :]
+    send, recv = rest[:2]
+    value, core_in, x_in, y_in, by_z = rest[2:7]
+    scratch = rest[7:]
+    place = Place()
+    links = Links(send, recv)
+    value[0] = error[...]
+    place.barrier()
+    total = Total(value, core_in, x_in, y_in, by_z, place, links)
+    work = [
+        Reduce(chunk, grads[i], outs[i], place, links, scratch[6 * i : 6 * i + 6])
+        for i, chunk in enumerate(chunks)
+    ]
+    total.step0()
+    work[0].step0()
+    swap = links.start(result, result_in, place.to_x)
+    for item in work[1:]:
+        item.step0()
+    total.step1()
+    for s in range(n + 4):
+        if s < 2:
+            getattr(total, "step" + str(s + 2))()
+        for i, item in enumerate(work):
+            if 0 <= s - i < 5:
+                getattr(item, "step" + str(s - i + 1))()
+    total_out[...] = total.step4()
+    swap.wait_recv()
+    links.drain()
+
+
+def reduce_all(chunks, grads, error, result):
+    bf16 = jnp.bfloat16
+    n = len(chunks)
+    out_shape = [jax.ShapeDtypeStruct((c.rows, c.cols), bf16) for c in chunks]
+    out_shape += [
+        jax.ShapeDtypeStruct((8, 128), jnp.float32),
+        jax.ShapeDtypeStruct(result.shape, bf16),
+    ]
+    copies = REDUCE_COPIES * n + TOTAL_COPIES + 1
+    small = pltpu.VMEM((8, 128), jnp.float32)
+    vmem = pl.BlockSpec(memory_space=pltpu.VMEM)
+    anywhere = pl.BlockSpec(memory_space=pl.ANY)
+    return pl.pallas_call(
+        functools.partial(reduce_kernel, chunks),
+        out_shape=out_shape,
+        in_specs=[vmem] * (n + 1) + [anywhere],
+        out_specs=[vmem] * (n + 1) + [anywhere],
+        scratch_shapes=[
+            pltpu.SemaphoreType.DMA((copies,)),
+            pltpu.SemaphoreType.DMA((copies,)),
+            pltpu.VMEM((3, 8, 128), jnp.float32),
+            small,
+            small,
+            small,
+            pltpu.VMEM((4, 8, 128), jnp.float32),
+        ]
+        + sum([reduce_scratch(c) for c in chunks], []),
+        compiler_params=pltpu.CompilerParams(
+            collective_id=1, has_side_effects=True, vmem_limit_bytes=56 * MIB
+        ),
+    )(*grads, error, result)
+
+
+def pick_rows(index, source):
+    chosen = index[:, None] == jnp.arange(source.shape[0], dtype=jnp.int32)[None, :]
+    return jnp.dot(
+        chosen.astype(jnp.bfloat16), source, preferred_element_type=jnp.float32
+    ).astype(jnp.bfloat16)
+
+
+def fused_shards(
+    tokens,
+    w_query,
+    w_key,
+    w_value,
+    w_out,
+    w_up,
+    w_down,
+    gain_attn,
+    gain_ffn,
+    teacher,
+    seq_lengths,
+    tok_perm,
+    valid_count,
+):
+    bf16, f32 = jnp.bfloat16, jnp.float32
+    rank = lax.axis_index("ctx")
+    dp_count = lax.axis_size("dp")
+    layer_in = tokens[0]
+    span, width = layer_in.shape
+    ff = w_up.shape[1]
+    shard = w_query.shape[0]
+    head_count = width // HEAD_DIM
+    order = tok_perm[0]
+    seq_len = order.shape[0]
+    length = seq_lengths[0]
+    counted = order < length
+    block = span // 2
+
+    def column_block(gain):
+        return jnp.pad(gain[:, None], ((0, 0), (0, 127)))
+
+    chunks = (
+        Chunk(shard, 3 * width, 640),
+        Chunk(shard, width + 256, 256),
+        Chunk(shard, ff, 896),
+        Chunk(w_down.shape[0], width, 256),
+    )
+    shards_in = (
+        jnp.concatenate([w_query, w_key, w_value], axis=1),
+        jnp.concatenate([w_out, column_block(gain_attn), column_block(gain_ffn)], axis=1),
+        w_up,
+        w_down,
+    )
+    by_block = order.reshape(2, 2, block)
+    mine_here = jnp.take(by_block, rank, axis=1)
+    own_pos = jnp.take(mine_here, rank, axis=0) - rank * span
+    peer_pos = jnp.take(mine_here, 1 - rank, axis=0) - rank * span
+    teach_own = pick_rows(own_pos, teacher[0])
+    teach_send = pick_rows(peer_pos, teacher[0])
+    qkv, out_gain, up_all, down_all, tokens_all, teach_in = gather_all(
+        chunks, shards_in, layer_in, teach_send
+    )
+    qkv = qkv.reshape(width, 3 * width)
+    out_gain = out_gain.reshape(width, width + 256)
+    up_weight = up_all.reshape(width, ff)
+    down_weight = down_all.reshape(ff, width)
+    out_weight = out_gain[:, :width]
+    gain_first = out_gain[:, width].astype(f32)
+    gain_second = out_gain[:, width + 128].astype(f32)
+    both = tokens_all.reshape(seq_len, width)
+    teach_dealt = jnp.where(
+        rank == 0,
+        jnp.concatenate([teach_own, teach_in]),
+        jnp.concatenate([teach_in, teach_own]),
+    ).astype(f32)
+
+    def project(rows, which):
+        return jnp.dot(
+            rows, qkv[:, which * width : (which + 1) * width], preferred_element_type=f32
+        ).astype(bf16)
+
+    queries = project(layer_in, 0).reshape(span, head_count, HEAD_DIM)
+    keys = project(both, 1).reshape(seq_len, head_count, HEAD_DIM)
+    values = project(both, 2).reshape(seq_len, head_count, HEAD_DIM)
+    scores = jnp.einsum("qhe,khe->hqk", queries, keys, preferred_element_type=f32) * SCORE_SCALE
+    scores = jnp.where(counted[None, None, :], scores, MASKED)
+    top = jnp.max(scores, axis=-1, keepdims=True)
+    weights = jnp.exp(scores - top)
+    total = jnp.sum(weights, axis=-1)
+    mixed = jnp.einsum("hqk,khe->hqe", weights.astype(bf16), values, preferred_element_type=f32)
+    log_total = top[..., 0] + jnp.log(total)
+    attn_full = jnp.transpose(mixed / total[..., None], (1, 0, 2)).reshape(span, width)
+    attn_low = attn_full.astype(bf16)
+    branch = jnp.dot(attn_low, out_weight, preferred_element_type=f32)
+    normed, normal_first, inverse_first = norm_forward(layer_in.astype(f32) + branch, gain_first)
+    normed_low = normed.astype(bf16)
+    upward = jnp.dot(normed_low, up_weight, preferred_element_type=f32)
+    active, gelu_pull = jax.vjp(gelu_exact, upward)
+    active_low = active.astype(bf16)
+    down_out = jnp.dot(active_low, down_weight, preferred_element_type=f32)
+    result, normal_second, inverse_second = norm_forward(normed + down_out, gain_second)
+    result_low = result.astype(bf16)
+    own_order = lax.dynamic_slice_in_dim(order, rank * span, span)
+    live = (own_order < length)[:, None]
+    error = jnp.where(live, result_low.astype(f32) - teach_dealt, 0.0)
+    square = jnp.sum(error * error)
+    valid_total = valid_count[0].astype(f32)
+    grad_scale = seq_len * dp_count / valid_total
+    grad_result = (error * grad_scale).astype(bf16).astype(f32)
+    grad_sum_second, grad_gain_second = norm_backward(
+        grad_result, gain_second, normal_second, inverse_second
+    )
+    down_grad_low = grad_sum_second.astype(bf16)
+    grad_down_w = row_product(active_low, down_grad_low)
+    grad_active = by_transpose(down_grad_low, down_weight)
+    grad_upward = gelu_pull(grad_active)[0].astype(bf16)
+    grad_up_w = row_product(normed_low, grad_upward)
+    grad_normed = grad_sum_second + by_transpose(grad_upward, up_weight)
+    grad_hidden, grad_gain_first = norm_backward(
+        grad_normed, gain_first, normal_first, inverse_first
+    )
+    branch_grad = grad_hidden.astype(bf16)
+    grad_out_w = row_product(attn_low, branch_grad)
+    attn_grad_low = by_transpose(branch_grad, out_weight).astype(bf16)
+    grad_heads = attn_grad_low.reshape(span, head_count, HEAD_DIM)
+    row_delta = jnp.sum(
+        (attn_grad_low.astype(f32) * attn_full).reshape(span, head_count, HEAD_DIM), axis=-1
+    ).T
+    scores = jnp.einsum("qhe,khe->hqk", queries, keys, preferred_element_type=f32) * SCORE_SCALE
+    soft = jnp.where(counted[None, None, :], jnp.exp(scores - log_total[..., None]), 0.0)
+    prob_grad = jnp.einsum("qhe,khe->hqk", grad_heads, values, preferred_element_type=f32)
+    score_grad = (soft * (prob_grad - row_delta[..., None])).astype(bf16)
+    value_grad = jnp.einsum("hqk,qhe->khe", soft.astype(bf16), grad_heads, preferred_element_type=f32)
+    query_grad = SCORE_SCALE * jnp.einsum("hqk,khe->qhe", score_grad, keys, preferred_element_type=f32)
+    key_grad = SCORE_SCALE * jnp.einsum("hqk,qhe->khe", score_grad, queries, preferred_element_type=f32)
+    both_grads = jnp.concatenate(
+        [key_grad.reshape(seq_len, width), value_grad.reshape(seq_len, width)], axis=1
+    )
+    theirs = lax.dynamic_slice_in_dim(both_grads, (1 - rank) * span, span).astype(bf16)
+    arrived = lax.ppermute(theirs, "ctx", [(0, 1), (1, 0)])
+    kv_grad = (
+        lax.dynamic_slice_in_dim(both_grads, rank * span, span) + arrived.astype(f32)
+    ).astype(bf16)
+    qkv_grad = jnp.concatenate([query_grad.reshape(span, width).astype(bf16), kv_grad], axis=1)
+    grad_qkv_w = row_product(layer_in, qkv_grad)
+    token_grad = grad_hidden + by_transpose(qkv_grad, qkv)
+    whole_grads = [
+        grad_qkv_w,
+        jnp.concatenate(
+            [grad_out_w, column_block(grad_gain_first), column_block(grad_gain_second)], axis=1
+        ),
+        grad_up_w,
+        grad_down_w,
+    ]
+    whole_grads = [
+        g.astype(bf16).reshape(4, 2, 2, c.rows, c.cols) for g, c in zip(whole_grads, chunks)
+    ]
+    result_send = lax.dynamic_slice_in_dim(result_low, (1 - rank) * block, block)
+    result_own = lax.dynamic_slice_in_dim(result_low, rank * block, block)
+    down_sum, up_sum, out_sum, qkv_sum, square_sum, result_in = reduce_all(
+        (chunks[3], chunks[2], chunks[1], chunks[0]),
+        (whole_grads[3], whole_grads[2], whole_grads[1], whole_grads[0]),
+        jnp.full((8, 128), square, f32),
+        result_send,
+    )
+    loss = (square_sum[0, 0] / (2.0 * width * valid_total)).reshape(1)
+    placed = jnp.concatenate([own_pos, peer_pos])
+    rows = jnp.arange(span, dtype=jnp.int32)
+    in_order = jnp.dot(
+        (rows[:, None] == placed[None, :]).astype(bf16),
+        jnp.concatenate([result_own, result_in]),
+        preferred_element_type=f32,
+    ).astype(bf16)
+    qkv_sum, out_sum = qkv_sum.astype(f32), out_sum.astype(f32)
+    return (
+        in_order[None],
+        loss,
+        token_grad[None],
+        qkv_sum[:, :width],
+        qkv_sum[:, width : 2 * width],
+        qkv_sum[:, 2 * width :],
+        out_sum[:, :width],
+        up_sum.astype(f32),
+        down_sum.astype(f32),
+        out_sum[:, width],
+        out_sum[:, width + 128],
+    )
+
+
 def solution(mesh):
     in_specs = (
         P("dp", "ctx", None),
@@ -347,4 +944,5 @@
         P("dp"),
         P("dp"),
     )
-    return jax.shard_map(shards, mesh=mesh, in_specs=in_specs, out_specs=out_specs, check_vma=False)
+    body = fused_shards if dict(mesh.shape) == {"dp": 16, "ctx": 2} else shards
+    return jax.shard_map(body, mesh=mesh, in_specs=in_specs, out_specs=out_specs, check_vma=False)

time: 989 us -> 405 us (0.41)
  waiting for transfers between devices: 596 us -> 8.94 us
  Pallas kernels: 0 us -> 196 us
  blocking collectives: 107 us -> 0 us
  local copies, waits for them, and re-layouts: 79.1 us -> 21.2 us
  between operations: 19.2 us -> 4.76 us
    reduce_scatter x5 -> x0, waiting for transfers between devices: 256 us -> none  [the longest x1 78.9 us: shards(): lax.psum_scatter(grad_down_w.astype(jnp.bfloat16), 'dp', scatter_dimensio...]
    all_gather x8 -> x0, waiting for transfers between devices: 197 us -> none  [the longest x1 45.6 us: shards(): lax.all_gather(w_down, 'dp', axis=0, tiled=True)]
    pallas_call x0 -> x2, Pallas kernels: none -> 196 us  [the longest x1 106 us: reduce_all(): pl.pallas_call(functools.partial(reduce_kernel, chunks), out_shape=out_sh...]
    unnamed x20 -> x0, waiting for transfers between devices: 120 us -> none
    unnamed x2 -> x0, blocking collectives: 62 us -> none
    psum x2 -> x0, blocking collectives: 44.6 us -> none  [the longest x1 39.7 us: shards(): total_sq = lax.psum(jnp.sum(residual_err * residual_err), ('dp', 'ctx'))]
    unnamed x84 -> x126, local copies, waits for them, and re-layouts: 30.8 us -> 4.37 us
    all_to_all x2 -> x0, waiting for transfers between devices: 18.9 us -> none  [the longest x1 11.4 us: shards(): lax.all_to_all(result_low, 'ctx', split_axis=0, concat_axis=0, tiled=True)]
  transfers between devices with their start and end apart: 19 -> 1, of which waited for: 16 -> 1; matrix products, arithmetic and copies ran while one was open for 14% -> 7% of each run, Pallas kernels for 0% -> 0%
where the time goes in v1:
time: 405 us; the launch traced here: 400 us
  Pallas kernels  196 us (48%)
  matrix products  129 us (32%)
  other arithmetic  38.7 us (10%)
  local copies, waits for them, and re-layouts  21.2 us (5%)
  waiting for transfers between devices  8.94 us (2%)
  between operations  4.76 us (1%)
    pallas_call x1, Pallas kernels, reduce_all(): pl.pallas_call(functools.partial(reduce_kernel, chunks), out_shape=out_sh...  106 us
    pallas_call x1, Pallas kernels, gather_all(): pl.pallas_call(functools.partial(gather_kernel, chunks), out_shape=out_sh...  90.3 us
    dot_general x4, matrix products, by_transpose(): lax.dot_general(left_mat, right_mat, (((1,), (1,)), ((), ())), preferred_...  19.8 us
    dot_general x4, matrix products, row_product(): lax.dot_general(left_mat, right_mat, (((0,), (0,)), ((), ())), preferred_...  16.8 us
    dot_general x1, matrix products, fused_shards(): jnp.einsum('qhe,khe->hqk', grad_heads, values, preferred_element_type=f32)  16.7 us
    dot_general x1, matrix products, fused_shards(): jnp.einsum('hqk,qhe->khe', soft.astype(bf16), grad_heads, preferred_eleme...  12.2 us
    reduce_sum x1, other arithmetic, fused_shards(): total = jnp.sum(weights, axis=-1)  11.3 us
    dot_general x1, matrix products, fused_shards(): jnp.einsum('hqk,khe->hqe', weights.astype(bf16), values, preferred_elemen...  10.6 us
  transfers between devices with their start and end apart: 1, of which 1 were waited for; matrix products, arithmetic and copies ran while one was open for 7% of the time, Pallas kernels for 0%

profile of v1, /device:TPU:0, one launch (start us, length us, event | category | flops | bytes accessed | tf_op | source)
XLA Modules:
  0.0 399.8 jit_solution(2814904457041500088)
XLA Ops:
  0.7 0.5 broadcast.208
  1.2 1.3 reduce.15
  2.6 0.8 copy.29
  3.4 0.8 copy.30
  4.1 0.5 broadcast_subtract_fusion
  4.7 1.2 convolution_convert_fusion.10.refs_5_
  5.8 1.7 pad_maximum_fusion.6.refs_0_
  7.6 0.6 fusion.50.refs_1_
  8.2 90.3 %shard_map.212 = (bf16[4,2,2,48,2304]{4,3,2,1,0:T(8,128)(2,1)}, bf16[4,2,2,48,1024]{4,3,2,1,0:T(8,128)(2,1)}, bf16[4,2,2,48,3072]{4,3,2,1,0:T(8,128)(2,1)}, bf16...) custom-call(bf16[48,2304]{1,0:T(8,128)(2,1)} %pad_maximum_fusion.6.refs_0_, ...), custom_call_target="tpu_custom_call" | custom-call | tf_op jit(solution)/shard_map/pallas_call | solution.py:650
  98.6 2.2 convolution_convert_fusion.7
  100.9 3.0 convolution_convert_fusion.4
  104.0 2.6 convolution_convert_fusion.3
  107.2 10.4 %select_reduce_fusion = (f32[12,512]{1,0:T(8,128)S(1)}, f32[12,512,1024]{2,1,0:T(8,128)}) fusion(pred[1024]{0:T(1024)(128)(4,1)S(1)} %compare_reduce_fusion, bf16[512,12,64]{0,2,1:T(8,128)(2,1)S(1)} %bitcast.104, bf16[1024,12,64]{0,2,1:T(8,128)(2,1)S(1)} %bitcast.100), kind=kOutput, calls=%fused_computation.3 | convolution fusion | flops 824174592 | bytes 27550720 | tf_op jit(solution)/shard_map/qhe,khe->hqk/dot_general | solution.py:813
  117.6 11.3 %fusion = f32[12,512]{1,0:T(8,128)S(1)} fusion(f32[12,512,1024]{2,1,0:T(8,128)} %get-tuple-element.78, f32[12,512]{1,0:T(8,128)S(1)} %get-tuple-element.77, pred[1024]{0:T(1024)(128)(4,1)S(1)} %compare_reduce_fusion), kind=kLoop, calls=%fused_computation.4 | loop fusion | flops 25159680 | bytes 25216000 | tf_op jit(solution)/shard_map/reduce_sum | solution.py:817
  129.0 0.6 log_add_fusion
  129.6 10.6 %bitcast_divide_fusion = f32[512,12,64]{0,2,1:T(8,128)S(1)} fusion(bf16[1024,12,64]{0,2,1:T(8,128)(2,1)S(1)} %bitcast.138, f32[12,512,1024]{2,1,0:T(8,128)} %get-tuple-element.78, f32[12,512]{1,0:T(8,128)S(1)} %get-tuple-element.77, pred[1024]{0:T(1024)(128)(4,1)S(1)} %compare_reduce_fusion, f32[512,12]{0,1:T(8,128)S(1)} %bitcast.118), kind=kOutput, calls=%fused_computation.40 | convolution fusion | flops 830865408 | bytes 28361728 | tf_op jit(solution)/shard_map/hqk,khe->hqe/dot_general | solution.py:818
  140.3 2.1 copy-done.16
  142.7 0.9 fusion.65
  143.6 0.3 multiply_reduce_fusion.4
  143.9 0.8 add_rsqrt_fusion.1
  144.9 6.7 %multiply_convert_fusion.1 = (bf16[512,3072]{1,0:T(8,128)(2,1)S(1)}, f32[512,3072]{1,0:T(8,128)}) fusion(bf16[768,3072]{1,0:T(8,128)(2,1)} %bitcast.125, f32[512,768]{1,0:T(8,128)S(1)} %get-tuple-element.80, f32[768]{0:T(1024)S(1)} %convert_reduce_fusion.1, f32[512]{0:T(512)} %add_rsqrt_fusion.1, f32[512]{0:T(512)S(1)} %broadcast_multiply_fusion.5), kind=kOutput, calls=%fused_computation.16 | convolution fusion | flops 2425356288 | bytes 15735808 | tf_op jit(solution)/shard_map/dot_general | solution.py:825
  151.6 6.7 %fusion.66 = (f32[512]{0:T(512)S(1)}, f32[512,768]{1,0:T(8,128)S(1)}) fusion(bf16[512,3072]{1,0:T(8,128)(2,1)S(1)} %get-tuple-element.81, bf16[3072,768]{1,0:T(8,128)(2,1)} %bitcast.129, f32[768]{0:T(1024)S(1)} %convert_reduce_fusion.1, f32[512]{0:T(512)S(1)} %copy-done.41, f32[512,768]{1,0:T(8,128)} %copy-done.7, f32[512]{0:T(512)S(1)} %broadcast_multiply_fusion.5), kind=kOutput, calls=%fused_computation.142 | convolution fusion | flops 2417884672 | bytes 11019264 | tf_op jit(solution)/shard_map/dot_general | solution.py:828
  158.3 0.3 multiply_reduce_fusion.3
  158.5 0.8 add_rsqrt_fusion
  159.5 1.0 convolution_convert_fusion.9
  161.3 4.5 %multiply_reduce_fusion = (f32[]{:T(128)}, f32[512]{0:T(512)S(1)}, bf16[768]{0:T(1024)(128)(2,1)}, f32[512]{0:T(512)S(1)}, bf16[512,768]{1,0:T(8,128)(2,1)}) fusion(pred[512]{0:T(512)(128)(4,1)S(1)} %compare_reduce_fusion.1, bf16[256,768]{1,0:T(8,128)(2,1)S(1)} %convolution_convert_fusion.9, bf16[256,768]{1,0:T(8,128)(2,1)} %get-tuple-element.29, ...), kind=kLoop, calls=%fused_computation.42 | loop fusion | flops 11008255 | bytes 3159049 | tf_op jit(solution)/shard_map/reduce_sum | solution.py:834
  165.9 9.5 %add_convert_fusion = bf16[512,3072]{1,0:T(8,128)(2,1)S(1)} fusion(f32[512,3072]{1,0:T(8,128)} %get-tuple-element.82, bf16[3072,768]{1,0:T(8,128)(2,1)} %bitcast.130, f32[512,768]{1,0:T(8,128)S(1)} %get-tuple-element.84, f32[512]{0:T(512)S(1)} %broadcast_multiply_fusion.2, f32[512]{0:T(512)S(1)} %broadcast_multiply_fusion.3, f32[]{:T(128)} %bitcast.19, ...), kind=kOutput, calls=%fused_computation.15 | convolution fusion | flops 2446589952 | bytes 16526853 | tf_op jit(solution)/shard_map/dot_general | solution.py:49
  175.5 5.1 %multiply_reduce_fusion.2 = (f32[512]{0:T(512)S(1)}, bf16[768]{0:T(1024)(128)(2,1)}, f32[512]{0:T(512)S(1)}, f32[512,768]{1,0:T(8,128)}) fusion(f32[512,768]{1,0:T(8,128)S(1)} %copy-done.8, f32[768]{0:T(1024)S(1)} %copy-done.32, f32[512]{0:T(512)S(1)} %copy-done.42, f32[512]{0:T(512)S(1)} %broadcast_multiply_fusion.5, ...), kind=kOutput, calls=%fused_computation.47 | convolution fusion | flops 2429286656 | bytes 13393925 | tf_op jit(solution)/shard_map/dot_general | solution.py:49
  180.7 3.0 copy.36
  183.7 2.5 subtract_multiply_fusion
  186.2 0.3 copy-done.17
  186.5 2.0 convert_multiply_fusion.2
  188.5 3.0 copy.37
  191.5 1.2 copy.35
  192.7 1.7 reduce_sum.128
  194.4 12.2 %fusion.3 = f32[12,64,1024]{2,1,0:T(8,128)} fusion(bf16[512,12,64]{0,2,1:T(8,128)(2,1)S(1)} %bitcast.115, f32[12,512,1024]{2,1,0:T(8,128)} %get-tuple-element.78, f32[12,512]{1,0:T(8,128)S(1)} %copy-done.29, pred[1024]{0:T(1024)(128)(4,1)S(1)} %copy-done.34), kind=kOutput, calls=%fused_computation.7 | convolution fusion | flops 830472192 | bytes 29123584 | tf_op jit(solution)/shard_map/hqk,qhe->khe/dot_general | solution.py:861
  206.7 16.7 %multiply_convert_fusion = bf16[12,512,1024]{2,1,0:T(8,128)(2,1)} fusion(f32[12,512,1024]{2,1,0:T(8,128)} %get-tuple-element.78, f32[12,512]{1,0:T(8,128)S(1)} %bitcast.119, f32[12,512]{1,0:T(8,128)S(1)} %copy-done.29, pred[1024]{0:T(1024)(128)(4,1)S(1)} %copy-done.34, bf16[512,12,64]{0,2,1:T(8,128)(2,1)S(1)} %bitcast.116, bf16[1024,12,64]{0,2,1:T(8,128)(2,1)} %bitcast.137), kind=kOutput, calls=%fused_computation | convolution fusion | flops 843055104 | bytes 40158208 | tf_op jit(solution)/shard_map/qhe,khe->hqk/dot_general | solution.py:859
  223.4 8.6 %convolution_multiply_fusion = f32[12,64,1024]{2,1,0:T(8,128)} fusion(bf16[512,12,64]{0,2,1:T(8,128)(2,1)S(1)} %bitcast.105, bf16[12,512,1024]{2,1,0:T(8,128)(2,1)} %multiply_convert_fusion), kind=kOutput, calls=%fused_computation.32 | convolution fusion | flops 806092800 | bytes 16515072 | tf_op jit(solution)/shard_map/hqk,qhe->khe/dot_general | solution.py:863
  231.9 3.4 fusion.10
  235.3 0.6 collective-permute-start
  235.9 4.9 %convolution_convert_fusion.1 = bf16[768,3072]{1,0:T(8,128)(2,1)} fusion(bf16[512,3072]{1,0:T(8,128)(2,1)S(1)} %copy-done.58, f32[512,768]{1,0:T(8,128)S(1)} %copy-done.9, f32[768]{0:T(1024)S(1)} %copy-done.32, f32[512]{0:T(512)S(1)} %copy-done.43, f32[512]{0:T(512)S(1)} %broadcast_multiply_fusion.5), kind=kOutput, calls=%fused_computation.19 | convolution fusion | flops 2419851264 | bytes 9444352 | tf_op jit(solution)/shard_map/dot_general | solution.py:43
  240.8 0.8 convolution_convert_fusion.5
  241.6 0.2 broadcast_in_dim.117
  241.9 0.7 pad.18.clone
  242.7 0.7 pad.19.clone
  243.4 2.5 pad_maximum_fusion.1.refs_2_
  245.9 0.8 constant_dynamic-slice_fusion.4
  246.8 0.7 copy-done.5
  247.5 7.4 %convolution_convert_fusion.2 = bf16[3072,768]{1,0:T(8,128)(2,1)} fusion(bf16[512,3072]{1,0:T(8,128)(2,1)} %copy-done.56, f32[512,768]{1,0:T(8,128)S(1)} %copy-done.5, f32[512]{0:T(512)S(1)} %copy-done.48, f32[512]{0:T(512)S(1)} %copy-done.50, f32[]{:T(128)} %bitcast.19, f32[768]{0:T(1024)S(1)} %convert_reduce_fusion, f32[512]{0:T(512)S(1)} %copy-done.40, ...), kind=kOutput, calls=%fused_computation.20 | convolution fusion | flops 2428502016 | bytes 10235397 | tf_op jit(solution)/shard_map/dot_general | solution.py:43
  254.8 8.6 %multiply_convert_fusion.2 = bf16[12,64,512]{2,1,0:T(8,128)(2,1)S(1)} fusion(bf16[1024,12,64]{0,2,1:T(8,128)(2,1)S(1)} %bitcast.101, bf16[12,512,1024]{2,1,0:T(8,128)(2,1)} %multiply_convert_fusion), kind=kOutput, calls=%fused_computation.43 | convolution fusion | flops 806092800 | bytes 14942208 | tf_op jit(solution)/shard_map/hqk,khe->qhe/dot_general | solution.py:862
  263.5 8.9 %collective-permute-done = bf16[512,1536]{0,1:T(8,128)(2,1)} collective-permute-done((bf16[512,1536]{0,1:T(8,128)(2,1)}, bf16[512,1536]{0,1:T(8,128)(2,1)}, u32[]{:S(2)}, u32[]{:S(2)}) %collective-permute-start) | collective-permute-done | bytes 1572896 | tf_op jit(solution)/shard_map/ppermute | solution.py:868
  272.5 1.9 fusion.13
  274.4 3.2 add_bitcast_fusion
  277.6 3.8 convolution_convert_fusion
  281.4 1.2 broadcast_in_dim.111.refs_4_
  282.7 105.8 %shard_map.213 = (bf16[192,768]{1,0:T(8,128)(2,1)}, bf16[48,3072]{1,0:T(8,128)(2,1)}, bf16[48,1024]{1,0:T(8,128)(2,1)}, bf16[48,2304]{1,0:T(8,128)(2,1)}, f32[8,128]{1,0:T(8,128)}, /*index=5*/bf16[256,768]{1,0:T(8,128)(2,1)}) custom-call(bf16[4,2,2,192,768]{4,3,2,1,0:T(8,128)(2,1)} %bitcast.103, bf16[4,2,2,48,3072]{4,3,2,1,0:T(8,128)(2,1)} %bitcast.102, ...), custom_call_target="tpu_custom_call" | custom-call | tf_op jit(solution)/shard_map/pallas_call | solution.py:710
  388.5 1.0 convert_element_type.189
  389.5 1.6 slice.77
  391.1 1.8 convert_element_type.190
  392.9 0.9 convert_element_type.191
  393.7 0.8 fusion.64
  394.5 0.6 slice_reduce_fusion
  395.1 1.2 slice.45
  397.0 1.5 fusion.24
  (140 shorter events, 1.2 us)
Async XLA Ops:
  0.6 4.0 %copy-start = (bf16[1,512,768]{2,1,0:T(8,128)(2,1)S(1)}, bf16[1,512,768]{2,1,0:T(8,128)(2,1)}, u32[]{:S(2)}) copy-start(bf16[1,512,768]{2,1,0:T(8,128)(2,1)} %param.24) | copy-start | bytes 2359300
  0.7 6.9 %copy-start.28 = (bf16[48,768]{1,0:T(8,128)(2,1)S(1)}, bf16[48,768]{1,0:T(8,128)(2,1)}, u32[]{:S(2)}) copy-start(bf16[48,768]{1,0:T(8,128)(2,1)} %param.19) | copy-start | bytes 221188
  4.7 3.6 copy-start.35
  5.8 92.7 %copy-start.22 = (bf16[1,512,768]{2,1,0:T(8,128)(2,1)S(1)}, bf16[1,512,768]{2,1,0:T(8,128)(2,1)}, u32[]{:S(2)}) copy-start(bf16[1,512,768]{2,1,0:T(8,128)(2,1)} %param.15) | copy-start | bytes 2359300
  98.6 2.4 copy-start.51
  100.9 3.0 copy-start.53
  103.9 3.3 copy-start.11
  103.9 3.3 copy-start.30
  107.2 22.4 %copy-start.33 = (pred[1024]{0:T(1024)(128)(4,1)}, pred[1024]{0:T(1024)(128)(4,1)S(1)}, u32[]{:S(2)}) copy-start(pred[1024]{0:T(1024)(128)(4,1)S(1)} %compare_reduce_fusion) | copy-start | bytes 3076
  117.6 12.0 %copy-start.55 = (bf16[1024,768]{0,1:T(8,128)(2,1)S(1)}, bf16[1024,768]{0,1:T(8,128)(2,1)}, u32[]{:S(2)}) copy-start(bf16[1024,768]{0,1:T(8,128)(2,1)} %convolution_convert_fusion.3) | copy-start | bytes 4718596
  140.2 2.3 copy-start.6
  140.2 2.3 copy-start.16
  140.2 2.4 copy-start.23
  140.3 3.3 copy-start.13
  143.6 8.0 %copy-start.7 = (f32[512,768]{1,0:T(8,128)}, f32[512,768]{1,0:T(8,128)S(1)}, u32[]{:S(2)}) copy-start(f32[512,768]{1,0:T(8,128)S(1)} %get-tuple-element.80) | copy-start | bytes 4718596
  144.8 6.7 %copy-start.31 = (f32[768]{0:T(1024)}, f32[768]{0:T(1024)S(1)}, u32[]{:S(2)}) copy-start(f32[768]{0:T(1024)S(1)} %convert_reduce_fusion.1) | copy-start | bytes 9220
  144.9 6.7 %copy-start.41 = (f32[512]{0:T(512)S(1)}, f32[512]{0:T(512)}, u32[]{:S(2)}) copy-start(f32[512]{0:T(512)} %add_rsqrt_fusion.1) | copy-start | bytes 6148
  151.5 6.7 %copy-start.56 = (bf16[512,3072]{1,0:T(8,128)(2,1)}, bf16[512,3072]{1,0:T(8,128)(2,1)S(1)}, u32[]{:S(2)}) copy-start(bf16[512,3072]{1,0:T(8,128)(2,1)S(1)} %get-tuple-element.81) | copy-start | bytes 9437188
  158.2 17.2 %copy-start.4 = (f32[512,768]{1,0:T(8,128)}, f32[512,768]{1,0:T(8,128)S(1)}, u32[]{:S(2)}) copy-start(f32[512,768]{1,0:T(8,128)S(1)} %get-tuple-element.84) | copy-start | bytes 4718596
  160.5 14.9 %copy-start.18 = (bf16[256,768]{1,0:T(8,128)(2,1)}, bf16[256,768]{1,0:T(8,128)(2,1)S(1)}, u32[]{:S(2)}) copy-start(bf16[256,768]{1,0:T(8,128)(2,1)S(1)} %convolution_convert_fusion.9) | copy-start | bytes 1179652
  161.2 14.2 %copy-start.45 = (pred[512]{0:T(512)(128)(4,1)}, pred[512]{0:T(512)(128)(4,1)S(1)}, u32[]{:S(2)}) copy-start(pred[512]{0:T(512)(128)(4,1)S(1)} %compare_reduce_fusion.1) | copy-start | bytes 1540
  161.3 4.5 %copy-start.25 = (bf16[256,768]{1,0:T(8,128)(2,1)S(1)}, bf16[256,768]{1,0:T(8,128)(2,1)}, u32[]{:S(2)}) copy-start(bf16[256,768]{1,0:T(8,128)(2,1)} %get-tuple-element.29) | copy-start | bytes 1179652
  161.3 4.5 %copy-start.39 = (f32[512]{0:T(512)S(1)}, f32[512]{0:T(512)}, u32[]{:S(2)}) copy-start(f32[512]{0:T(512)} %add_rsqrt_fusion) | copy-start | bytes 6148
  161.3 14.1 %slice-start = ((s8[4718592]{0:T(1024)(128)(4,1)}), s8[4194304]{0:T(1024)(128)(4,1)S(1)}, s32[]{:S(2)}) async-start(s8[4718592]{0:T(1024)(128)(4,1)} %bitcast.126), calls=%async_computation | async-start | bytes 8388608
  165.8 9.6 %copy-start.47 = (f32[512]{0:T(512)}, f32[512]{0:T(512)S(1)}, u32[]{:S(2)}) copy-start(f32[512]{0:T(512)S(1)} %broadcast_multiply_fusion.2) | copy-start | bytes 6148
  165.8 9.6 %copy-start.49 = (f32[512]{0:T(512)}, f32[512]{0:T(512)S(1)}, u32[]{:S(2)}) copy-start(f32[512]{0:T(512)S(1)} %broadcast_multiply_fusion.3) | copy-start | bytes 6148
  165.9 9.6 %copy-start.8 = (f32[512,768]{1,0:T(8,128)S(1)}, f32[512,768]{1,0:T(8,128)}, u32[]{:S(2)}) copy-start(f32[512,768]{1,0:T(8,128)} %copy-done.7) | copy-start | bytes 4718596
  165.9 9.6 %copy-start.32 = (f32[768]{0:T(1024)S(1)}, f32[768]{0:T(1024)}, u32[]{:S(2)}) copy-start(f32[768]{0:T(1024)} %copy-done.31) | copy-start | bytes 9220
  165.9 9.6 %copy-start.42 = (f32[512]{0:T(512)S(1)}, f32[512]{0:T(512)}, u32[]{:S(2)}) copy-start(f32[512]{0:T(512)} %add_rsqrt_fusion.1) | copy-start | bytes 6148
  165.9 9.6 %slice-start.1 = ((s8[4718592]{0:T(1024)(128)(4,1)}), s8[524288]{0:T(1024)(128)(4,1)S(1)}, s32[]{:S(2)}) async-start(s8[4718592]{0:T(1024)(128)(4,1)} %bitcast.126), calls=%async_computation.1 | async-start | bytes 1048576
  175.5 5.2 %copy-start.57 = (bf16[512,3072]{1,0:T(8,128)(2,1)}, bf16[512,3072]{1,0:T(8,128)(2,1)S(1)}, u32[]{:S(2)}) copy-start(bf16[512,3072]{1,0:T(8,128)(2,1)S(1)} %add_convert_fusion) | copy-start | bytes 9437188
  183.7 2.5 copy-start.10
  183.7 2.8 copy-start.17
  191.5 2.9 copy-start.29
  191.5 2.9 copy-start.34
  192.7 1.7 copy-start.21
  231.9 4.0 copy-start.9
  231.9 4.0 copy-start.43
  231.9 4.0 copy-start.58
  235.3 5.4 %copy-start.14 = (bf16[512,768]{0,1:T(8,128)(2,1)S(1)}, bf16[512,768]{0,1:T(8,128)(2,1)}, u32[]{:S(2)}) copy-start(bf16[512,768]{0,1:T(8,128)(2,1)} %copy-done.13) | copy-start | bytes 2359300
  235.3 37.1 %collective-permute-start = (bf16[512,1536]{0,1:T(8,128)(2,1)}, bf16[512,1536]{0,1:T(8,128)(2,1)}, u32[]{:S(2)}, u32[]{:S(2)}) collective-permute-start(bf16[512,1536]{0,1:T(8,128)(2,1)} %fusion.10), channel_id=1, source_target_pairs={{0,1},{1,0},{2,3},{3,2},{4,5},{5,4},{6,7},{7,6},{8,9},{9,8},{10,11... | collective-permute-start | bytes 4718600 | tf_op jit(solution)/shard_map/ppermute | solution.py:868
  240.8 0.8 copy-start.44
  240.8 1.0 copy-start.38
  243.4 2.5 copy-start.15
  243.4 3.4 copy-start.19
  243.4 3.4 copy-start.26
  245.9 0.9 copy-start.36
  245.9 0.9 copy-start.37
  245.9 1.6 copy-start.5
  245.9 1.6 copy-start.40
  245.9 1.5 copy-start.46
  245.9 1.5 copy-start.48
  245.9 1.5 copy-start.50
  247.5 7.4 %copy-start.12 = (bf16[1024,768]{0,1:T(8,128)(2,1)S(1)}, bf16[1024,768]{0,1:T(8,128)(2,1)}, u32[]{:S(2)}) copy-start(bf16[1024,768]{0,1:T(8,128)(2,1)} %copy-done.11) | copy-start | bytes 4718596
  254.8 17.6 %copy-start.2 = (f32[12,64,1024]{2,1,0:T(8,128)S(1)}, f32[12,64,1024]{2,1,0:T(8,128)}, u32[]{:S(2)}) copy-start(f32[12,64,1024]{2,1,0:T(8,128)} %convolution_multiply_fusion) | copy-start | bytes 9437188
  254.8 17.6 %copy-start.3 = (f32[12,64,1024]{2,1,0:T(8,128)S(1)}, f32[12,64,1024]{2,1,0:T(8,128)}, u32[]{:S(2)}) copy-start(f32[12,64,1024]{2,1,0:T(8,128)} %fusion.3) | copy-start | bytes 9437188
  263.5 10.9 %copy-start.52 = (bf16[4,2,2,48,2304]{4,3,2,1,0:T(8,128)(2,1)S(1)}, bf16[4,2,2,48,2304]{4,3,2,1,0:T(8,128)(2,1)}, u32[]{:S(2)}) copy-start(bf16[4,2,2,48,2304]{4,3,2,1,0:T(8,128)(2,1)} %get-tuple-element.24) | copy-start | bytes 10616836
  274.4 3.2 copy-start.24
  388.5 4.4 %copy-start.27 = (bf16[192,768]{1,0:T(8,128)(2,1)S(1)}, bf16[192,768]{1,0:T(8,128)(2,1)}, u32[]{:S(2)}) copy-start(bf16[192,768]{1,0:T(8,128)(2,1)} %get-tuple-element.35) | copy-start | bytes 884740
  388.5 5.3 %copy-start.20 = (bf16[48,2304]{1,0:T(8,128)(2,1)S(1)}, bf16[48,2304]{1,0:T(8,128)(2,1)}, u32[]{:S(2)}) copy-start(bf16[48,2304]{1,0:T(8,128)(2,1)} %get-tuple-element.32) | copy-start | bytes 663556
  389.4 7.5 %copy-start.54 = (bf16[256,768]{1,0:T(8,128)(2,1)S(1)}, bf16[256,768]{1,0:T(8,128)(2,1)}, u32[]{:S(2)}) copy-start(bf16[256,768]{1,0:T(8,128)(2,1)} %get-tuple-element.30) | copy-start | bytes 1179652
  393.7 4.7 %copy-start.1 = (bf16[1,512,768]{2,1,0:T(8,128)(2,1)S(1)}, bf16[1,512,768]{2,1,0:T(8,128)(2,1)}, u32[]{:S(2)}) copy-start(bf16[1,512,768]{2,1,0:T(8,128)(2,1)} %param.24) | copy-start | bytes 2359300

commit v2 on v0

--- a/solution.py
+++ b/solution.py
@@ -1,8 +1,11 @@
+import functools
 import math
 
 import jax
 import jax.numpy as jnp
 from jax import lax
+from jax.experimental import pallas as pl
+from jax.experimental.pallas import tpu as pltpu
 from jax.sharding import PartitionSpec as P
 
 HEAD_DIM = 64
@@ -11,6 +14,8 @@
 EPSILON = 1e-06
 SCORE_SCALE = 0.125
 MASKED = -1e30
+MESH = pl.DeviceIdType.MESH
+MIB = 1024 * 1024
 
 
 def gelu_exact(values):
@@ -318,6 +323,976 @@
     )
 
 
+class Place:
+    def __init__(self):
+        dp = lax.axis_index("dp")
+        self.x = lax.axis_index("ctx")
+        self.z, self.y, self.c = dp // 4, (dp // 2) % 2, dp % 2
+        self.xo, self.yo, self.co = 1 - self.x, 1 - self.y, 1 - self.c
+        self.to_x = (dp, self.xo)
+        self.to_y = (self.z * 4 + self.yo * 2 + self.c, self.x)
+        self.to_c = (self.z * 4 + self.y * 2 + self.co, self.x)
+        self.z_up = [(self.z + k) % 4 for k in range(4)]
+        self.z_down = [(self.z + 4 - k) % 4 for k in range(4)]
+        self.to_z = [(self.z_up[k] * 4 + self.y * 2 + self.c, self.x) for k in range(4)]
+
+    def barrier(self):
+        semaphore = pltpu.get_barrier_semaphore()
+        for partner in [self.to_x, self.to_y, self.to_c] + self.to_z[1:]:
+            pl.semaphore_signal(semaphore, inc=1, device_id=partner, device_id_type=MESH)
+        pl.semaphore_wait(semaphore, 6)
+
+
+class Links:
+    def __init__(self, send, recv):
+        self.send, self.recv, self.used, self.all = send, recv, 0, []
+
+    def start(self, src, dst, partner):
+        at = self.used
+        self.used += 1
+        copy = pltpu.make_async_remote_copy(
+            src_ref=src,
+            dst_ref=dst,
+            send_sem=self.send.at[at],
+            recv_sem=self.recv.at[at],
+            device_id=partner,
+            device_id_type=MESH,
+        )
+        copy.start()
+        self.all.append(copy)
+        return copy
+
+    def sent(self, copy):
+        copy.wait_send()
+        self.all = [other for other in self.all if other is not copy]
+
+    def drain(self):
+        for copy in self.all:
+            copy.wait_send()
+
+
+class Cut:
+    def __init__(self, width, first):
+        self.full = width // 2
+        self.one, self.two = first, width // 2 - first
+
+    def half(self, x):
+        return pl.ds(pl.multiple_of(x * self.full, 128), self.full)
+
+    def first(self, x):
+        return pl.ds(pl.multiple_of(x * self.full, 128), self.one)
+
+    def second(self, x):
+        return pl.ds(pl.multiple_of(x * self.full + self.one, 128), self.two)
+
+
+class Gather:
+    copies = 23
+
+    def __init__(self, rows, cut, shard, whole, place, links, own_sem):
+        self.rows, self.cut, self.shard, self.whole = rows, cut, shard, whole
+        self.p, self.links = place, links
+        self.own = pltpu.make_async_copy(
+            shard.at[rows], whole.at[place.z, place.y, place.c, rows], own_sem
+        )
+
+    def piece(self, z, y, cols):
+        return self.whole.at[z, y, self.p.c, self.rows, cols]
+
+    def push(self, piece, partner):
+        return self.links.start(piece, piece, partner)
+
+    def step0(self):
+        p, rows = self.p, self.rows
+        mine = self.cut.half(p.x)
+        source, target = self.shard.at[rows, mine], self.piece(p.z, p.y, mine)
+        self.from_z = [self.links.start(source, target, p.to_z[k]) for k in range(1, 4)]
+        self.own.start()
+        self.from_y = [self.links.start(source, target, p.to_y)]
+        self.from_c = [
+            self.links.start(self.shard.at[rows], self.whole.at[p.z, p.y, p.c, rows], p.to_c)
+        ]
+
+    def step1(self):
+        p = self.p
+        self.from_x = []
+        for k in range(1, 4):
+            self.from_z[k - 1].wait_recv()
+            piece = self.piece(p.z_down[k], p.y, self.cut.half(p.x))
+            self.from_x.append(self.push(piece, p.to_x))
+            self.from_y.append(self.push(piece, p.to_y))
+            self.from_c.append(self.push(piece, p.to_c))
+
+    def step2(self):
+        p, cut, every = self.p, self.cut, slice(None)
+        self.own.wait()
+        for k in range(1, 4):
+            self.from_x[k - 1].wait_recv()
+        self.first_y = self.push(self.piece(every, p.y, cut.first(p.xo)), p.to_y)
+        for k in range(1, 4):
+            self.from_c.append(self.push(self.piece(p.z_down[k], p.y, cut.half(p.xo)), p.to_c))
+        for copy in self.from_y:
+            copy.wait_recv()
+        self.second_x = self.push(self.piece(every, p.yo, cut.second(p.x)), p.to_x)
+        self.from_c.append(self.push(self.piece(every, p.yo, cut.half(p.x)), p.to_c))
+
+    def step3(self):
+        p, cut, every = self.p, self.cut, slice(None)
+        self.first_y.wait_recv()
+        self.from_c.append(self.push(self.piece(every, p.yo, cut.first(p.xo)), p.to_c))
+        self.second_x.wait_recv()
+        self.from_c.append(self.push(self.piece(every, p.yo, cut.second(p.xo)), p.to_c))
+
+    def step4(self):
+        for copy in self.from_c:
+            copy.wait_recv()
+
+
+class Reduce:
+    copies = 10
+
+    def __init__(self, rows, at, first_row, cut, grads, out, place, links, scratch):
+        self.rows, self.cut, self.grads, self.out = rows, cut, grads, out
+        self.at, self.here = pl.ds(at, rows), pl.ds(first_row, rows)
+        self.at0, self.here0 = at, first_row
+        self.p, self.links = place, links
+        self.core_in, self.x_in, self.y_in, self.y_in2, self.x_in2, self.z_in = scratch
+        self.block = max(b for b in range(16, min(rows, 96) + 1, 16) if rows % b == 0)
+        self.stage = 0
+
+    def add(self, outer, target, source):
+        steps = self.rows // self.block
+
+        def body(i, carry):
+            first = pl.multiple_of((i % steps) * self.block, 16)
+            put = target(i // steps, pl.ds(self.at0 + first, self.block))
+            given = source(i // steps, pl.ds(self.here0 + first, self.block))
+            self.grads[put] = (
+                self.grads[put].astype(jnp.float32) + given.astype(jnp.float32)
+            ).astype(jnp.bfloat16)
+            return carry
+
+        lax.fori_loop(0, outer * steps, body, 0)
+
+    def step0(self):
+        p = self.p
+        self.by_core = self.links.start(
+            self.grads.at[:, :, p.co, self.at], self.core_in.at[:, :, self.here], p.to_c
+        )
+
+    def step1(self):
+        p, cut, grads = self.p, self.cut, self.grads
+        self.by_core.wait_recv()
+        self.add(
+            8,
+            lambda i, rows: (i // 2, i % 2, p.c, rows),
+            lambda i, rows: self.core_in[i // 2, i % 2, rows],
+        )
+        self.by_y = [
+            self.links.start(
+                grads.at[:, p.yo, p.c, self.at, cut.first(h)], self.y_in.at[h, :, self.here], p.to_y
+            )
+            for h in range(2)
+        ]
+        self.by_x = self.links.start(
+            grads.at[:, :, p.c, self.at, cut.second(p.xo)], self.x_in.at[:, :, self.here], p.to_x
+        )
+
+    def step2(self):
+        p, cut, grads = self.p, self.cut, self.grads
+        for h in range(2):
+            self.by_y[h].wait_recv()
+            self.add(
+                4,
+                lambda i, rows: (i, p.y, p.c, rows, cut.first(h)),
+                lambda i, rows: self.y_in[h, i, rows],
+            )
+        self.by_x2 = self.links.start(
+            grads.at[:, p.y, p.c, self.at, cut.first(p.xo)], self.x_in2.at[:, self.here], p.to_x
+        )
+        self.by_x.wait_recv()
+        self.add(
+            8,
+            lambda i, rows: (i // 2, i % 2, p.c, rows, cut.second(p.x)),
+            lambda i, rows: self.x_in[i // 2, i % 2, rows],
+        )
+        self.by_y2 = self.links.start(
+            grads.at[:, p.yo, p.c, self.at, cut.second(p.x)], self.y_in2.at[:, self.here], p.to_y
+        )
+
+    def step3(self):
+        p, cut, grads = self.p, self.cut, self.grads
+        self.by_x2.wait_recv()
+        self.add(
+            4,
+            lambda i, rows: (i, p.y, p.c, rows, cut.first(p.x)),
+            lambda i, rows: self.x_in2[i, rows],
+        )
+        self.by_y2.wait_recv()
+        self.add(
+            4,
+            lambda i, rows: (i, p.y, p.c, rows, cut.second(p.x)),
+            lambda i, rows: self.y_in2[i, rows],
+        )
+        self.by_z = [
+            self.links.start(
+                grads.at[p.z_up[k], p.y, p.c, self.at, cut.half(p.x)],
+                self.z_in.at[k - 1, self.here],
+                p.to_z[k],
+            )
+            for k in range(1, 4)
+        ]
+
+    def step4(self):
+        p, mine = self.p, self.cut.half(self.p.x)
+        for copy in self.by_z:
+            copy.wait_recv()
+
+        def body(i, carry):
+            first = pl.multiple_of(i * self.block, 16)
+            rows = pl.ds(self.here0 + first, self.block)
+            total = self.grads[p.z, p.y, p.c, pl.ds(self.at0 + first, self.block), mine].astype(
+                jnp.float32
+            )
+            for k in range(3):
+                total = total + self.z_in[k, rows].astype(jnp.float32)
+            self.out[rows, mine] = total.astype(jnp.bfloat16)
+            return carry
+
+        lax.fori_loop(0, self.rows // self.block, body, 0)
+        done = self.out.at[self.here, mine]
+        self.last = self.links.start(done, done, p.to_x)
+
+    def step5(self):
+        self.last.wait_recv()
+
+    def beat(self):
+        getattr(self, "step" + str(self.stage))()
+        self.stage += 1
+
+
+def reduce_scratch(rows, cut, width):
+    bf16 = jnp.bfloat16
+    return [
+        pltpu.VMEM((4, 2, rows, width), bf16),
+        pltpu.VMEM((4, 2, rows, cut.two), bf16),
+        pltpu.VMEM((2, 4, rows, cut.one), bf16),
+        pltpu.VMEM((4, rows, cut.two), bf16),
+        pltpu.VMEM((4, rows, cut.one), bf16),
+        pltpu.VMEM((3, rows, cut.full), bf16),
+    ]
+
+
+class Total:
+    copies = 6
+
+    def __init__(self, value, core_in, x_in, y_in, by_z, place, links):
+        self.value, self.core_in, self.x_in, self.y_in, self.by_z = value, core_in, x_in, y_in, by_z
+        self.p, self.links = place, links
+        self.stage = 0
+
+    def step0(self):
+        self.copy = self.links.start(self.value.at[0], self.core_in, self.p.to_c)
+
+    def step1(self):
+        self.copy.wait_recv()
+        self.value[1] = self.value[0] + self.core_in[...]
+        self.copy = self.links.start(self.value.at[1], self.x_in, self.p.to_x)
+
+    def step2(self):
+        self.copy.wait_recv()
+        self.value[2] = self.value[1] + self.x_in[...]
+        self.copy = self.links.start(self.value.at[2], self.y_in, self.p.to_y)
+
+    def step3(self):
+        self.copy.wait_recv()
+        z = self.p.z
+        self.by_z[z] = self.value[2] + self.y_in[...]
+        self.spread = [
+            self.links.start(self.by_z.at[z], self.by_z.at[z], self.p.to_z[k]) for k in range(1, 4)
+        ]
+
+    def step4(self):
+        for copy in self.spread:
+            copy.wait_recv()
+
+    def step5(self):
+        pass
+
+    def sum(self):
+        return ((self.by_z[0] + self.by_z[1]) + self.by_z[2]) + self.by_z[3]
+
+    def beat(self):
+        getattr(self, "step" + str(self.stage))()
+        self.stage += 1
+
+
+ROOT_HALF = 0.7071067811865476
+DENSITY = 0.3989422804014327
+
+
+def dot(left, right):
+    return jnp.dot(left, right, preferred_element_type=jnp.float32)
+
+
+def layer_kernel(s, *refs):
+    (tokens, packed, teacher, order_row, order_col, length, valid) = refs[:7]
+    (ordered_out, total_out, token_out, grads_out) = refs[7:11]
+    (W, G, tok, qs, ks, vs, dO, stat, attn, n1, r1, low1, act, gp, acc, teach, res_in, low2, gains, sums) = refs[11:31]
+    total_refs, (send, recv, local), scratch = refs[31:36], refs[36:39], refs[39:]
+    f32, bf16 = jnp.float32, jnp.bfloat16
+    span, width, shard, downs = s.span, s.width, s.shard, s.downs
+    pairs = width // 128
+    third = width // 3
+    half = width // 2
+    place = Place()
+    x, xo = place.x, place.xo
+    cut = s.cut
+    links = Links(send, recv)
+
+    def own(first, size):
+        return pl.ds(pl.multiple_of(x * span + first, 16), size)
+
+    def other(first, size):
+        return pl.ds(pl.multiple_of(xo * span + first, 16), size)
+
+    def loop(count, body):
+        def step(i, carry):
+            body(i)
+            return carry
+
+        lax.fori_loop(0, count, step, 0)
+
+    def by_columns(first, n):
+        cols = pl.ds(pl.multiple_of(n * third, 128), third)
+        rows = pl.ds(pl.multiple_of(first, 16), shard)
+        return W[:, :, :, rows, cols].reshape(width, third)
+
+    def half_rows(first, m):
+        rows = pl.ds(pl.multiple_of(first, 16), shard)
+        return W[pl.ds(2 * m, 2), :, :, rows, :].reshape(half, width)
+
+    def down_block(p, y):
+        return W[p, y, :, s.down0 : s.down0 + downs, :].reshape(2 * downs, width)
+
+    gathers = [
+        Gather(pl.ds(a, b - a), cut, packed, W, place, links, local.at[i])
+        for i, (a, b) in enumerate(s.gather_rows)
+    ]
+    n_gather = len(gathers)
+    order = sorted(
+        [(step + s.lag * i, i, step) for i in range(n_gather) for step in range(5)]
+    )
+    ready = [order.index(entry) for entry in order if entry[2] == 4]
+    done = [0]
+
+    def run_until(index):
+        while done[0] <= index:
+            entry = order[done[0]]
+            getattr(gathers[entry[1]], "step" + str(entry[2]))()
+            done[0] += 1
+
+    def tick(count):
+        run_until(min(done[0] + count, len(order)) - 1)
+
+    place.barrier()
+    own_tokens = pltpu.make_async_copy(tokens, tok.at[own(0, span)], local.at[n_gather])
+    own_tokens.start()
+    own_teacher = pltpu.make_async_copy(teacher, gp.at[0], local.at[n_gather + 1])
+    own_teacher.start()
+    run_until(0)
+    send_tokens = links.start(tokens, tok.at[own(0, span)], place.to_x)
+    length_now = length[0]
+    iota_rows = lax.broadcasted_iota(jnp.int32, (s.block, span), 1)
+
+    def pick(c):
+        rows = pl.ds(pl.multiple_of(c * span + x * s.block, 16), s.block)
+        position = order_col[rows, :] - x * span
+        chosen = iota_rows == jnp.concatenate([position] * (span // 128), axis=1)
+        return jnp.where(chosen, 1.0, 0.0).astype(bf16)
+
+    own_teacher.wait()
+    for n in range(3):
+        cols = slice(n * third, (n + 1) * third)
+        gp[1, : s.block, cols] = dot(pick(xo), gp[0, :, cols]).astype(bf16)
+        teach[x, :, cols] = dot(pick(x), gp[0, :, cols]).astype(bf16)
+    run_until(ready[0])
+    teach_copy = links.start(gp.at[1, pl.ds(0, s.block)], teach.at[x], place.to_x)
+
+    own_tokens.wait()
+
+    def project(rows, which):
+        def body(n):
+            cols = pl.ds(pl.multiple_of(n * third, 128), third)
+            for first, target, scale in which:
+                value = dot(tok[rows, :], by_columns(first, n)).astype(bf16)
+                target[rows, cols] = value * scale if scale != 1.0 else value
+
+        loop(3, body)
+
+    sets = ((0, qs, SCORE_SCALE), (shard, ks, 1.0), (2 * shard, vs, 1.0))
+    project(own(0, span), sets)
+    tick(s.tick_project)
+    send_tokens.wait_recv()
+    project(other(0, span), sets)
+    tick(s.tick_project)
+
+    lane = lax.broadcasted_iota(jnp.int32, (1, 128), 1)
+    even32 = lane < HEAD_DIM
+    even = jnp.where(even32, 1.0, 0.0).astype(bf16)
+    odd = jnp.where(even32, 0.0, 1.0).astype(bf16)
+    bias_row = jnp.where(order_row[0:1, :] < length_now, 0.0, MASKED)
+    rows_q = s.rows_q
+
+    def attend(pair):
+        lanes = pl.ds(pair * 128, 128)
+
+        def body(b):
+            rows = own(b * rows_q, rows_q)
+            query, key, value = qs[rows, lanes], ks[:, lanes], vs[:, lanes]
+            tops, mixed = [], []
+            for keep, rest in ((even, odd), (odd, even)):
+                scores = (
+                    lax.dot_general(
+                        query * keep, key, (((1,), (1,)), ((), ())), preferred_element_type=f32
+                    )
+                    + bias_row
+                )
+                top = jnp.max(scores, axis=1, keepdims=True)
+                weight = jnp.exp(scores - top).astype(bf16)
+                tops.append(top)
+                mixed.append(dot(weight, value * keep + rest))
+            part = jnp.where(even32, mixed[0], mixed[1])
+            total = pltpu.roll(jnp.where(even32, mixed[1], mixed[0]), HEAD_DIM, 1)
+            out = pl.ds(pl.multiple_of(b * rows_q, 16), rows_q)
+            attn[out, lanes] = (part / total).astype(bf16)
+            log_total = jnp.where(even32, tops[0], tops[1]) + jnp.log(total)
+            log_rows = log_total.T
+            for h in range(2):
+                stat[x, 0, pl.ds(2 * pair + h, 1), pl.ds(pl.multiple_of(b * rows_q, 128), rows_q)] = (
+                    log_rows[h * HEAD_DIM : h * HEAD_DIM + 1, :]
+                )
+
+        loop(span // rows_q, body)
+
+    for pair in range(pairs):
+        attend(pair)
+        tick(s.tick_attend)
+
+    run_until(ready[1])
+    device = lax.broadcasted_iota(jnp.int32, (16, width), 0)
+    feature = lax.broadcasted_iota(jnp.int32, (16, width), 1)
+    mine = (feature // shard) == device
+    spread = jnp.where(
+        lax.broadcasted_iota(jnp.int32, (128, width), 1) % shard
+        == lax.broadcasted_iota(jnp.int32, (128, width), 0),
+        1.0,
+        0.0,
+    ).astype(bf16)
+    gain_rows = W[:, :, :, s.gain0 : s.gain0 + 16, :128].reshape(16, 16, 128).astype(f32)
+    for g in range(2):
+        wide = dot(gain_rows[:, g, :].astype(bf16), spread)
+        gains[g : g + 1, :] = jnp.sum(jnp.where(mine, wide, 0.0), axis=0, keepdims=True)
+
+    def branch(n):
+        cols = pl.ds(pl.multiple_of(n * third, 128), third)
+        acc[:, cols] = dot(attn[...], by_columns(s.out0, n))
+
+    loop(3, branch)
+    rows_n = s.rows_n
+
+    def wide_column(column):
+        return jnp.broadcast_to(column, (rows_n, 128))
+
+    def first_norm(b):
+        first = pl.multiple_of(b * rows_n, 16)
+        rows = pl.ds(first, rows_n)
+        hidden = tok[own(first, rows_n), :].astype(f32) + acc[rows, :]
+        center = hidden - jnp.mean(hidden, axis=1, keepdims=True)
+        inverse = lax.rsqrt(jnp.mean(center * center, axis=1, keepdims=True) + EPSILON)
+        normal = center * inverse
+        n1[rows, :] = normal
+        r1[rows, :] = wide_column(inverse)
+        low1[rows, :] = (normal * gains[0:1, :]).astype(bf16)
+
+    loop(span // rows_n, first_norm)
+    tick(s.tick_norm)
+
+    teach_copy.wait_recv()
+    links.sent(teach_copy)
+    run_until(ready[s.up_ready])
+
+    def upward(t):
+        p, n = t // 3, t % 3
+        cols = pl.ds(pl.multiple_of(n * third, 128), third)
+        value = dot(low1[...], by_columns(s.up0 + p * shard, n))
+        cdf = 0.5 * (1.0 + lax.erf(value * ROOT_HALF))
+        act[p, :, cols] = (value * cdf).astype(bf16)
+        gp[p, :, cols] = (cdf + value * (jnp.exp(-0.5 * value * value) * DENSITY)).astype(bf16)
+
+    loop(3 * s.panels, upward)
+    run_until(len(order) - 1)
+
+    def downward(n):
+        cols = pl.ds(pl.multiple_of(n * third, 128), third)
+        value = None
+        for p in range(s.panels):
+            weight = W[p, :, :, s.down0 : s.down0 + downs, cols].reshape(width, third)
+            part = dot(act[p], weight)
+            value = part if value is None else value + part
+        acc[:, cols] = value
+
+    loop(3, downward)
+
+    sums[...] = jnp.zeros_like(sums)
+    valid_total = jnp.full((1, 1), valid[0], jnp.int32).astype(f32)
+    grad_scale = s.tokens / valid_total
+
+    def fold(values):
+        return jnp.sum(values.reshape(rows_n // 8, 8, width), axis=0)
+
+    def second_norm(b):
+        first = pl.multiple_of(b * rows_n, 16)
+        rows = pl.ds(first, rows_n)
+        hidden = n1[rows, :] * gains[0:1, :] + acc[rows, :]
+        center = hidden - jnp.mean(hidden, axis=1, keepdims=True)
+        inverse = lax.rsqrt(jnp.mean(center * center, axis=1, keepdims=True) + EPSILON)
+        normal = center * inverse
+        gain = gains[1:2, :]
+        result = (normal * gain).astype(bf16)
+        per = s.block // rows_n
+        at = pl.ds(pl.multiple_of((b % per) * rows_n, 16), rows_n)
+        target = teach[b // per, at, :].astype(f32)
+        teach[b // per, at, :] = result
+        live = order_col[own(first, rows_n), 0:1] < length_now
+        error = jnp.where(live, result.astype(f32) - target, 0.0)
+        sums[2] += fold(error * error)
+        grad = (error * grad_scale).astype(bf16).astype(f32)
+        sums[1] += fold(grad * normal)
+        scaled = grad * gain
+        grad_sum = inverse * (
+            scaled
+            - jnp.mean(scaled, axis=1, keepdims=True)
+            - normal * jnp.mean(scaled * normal, axis=1, keepdims=True)
+        )
+        acc[rows, :] = grad_sum
+        low2[rows, :] = grad_sum.astype(bf16)
+
+    loop(span // rows_n, second_norm)
+    links.drain()
+    links.all = []
+    send_result = links.start(teach.at[xo], res_in, place.to_x)
+    total_refs[0][0] = jnp.broadcast_to(
+        jnp.sum(jnp.sum(sums[2], axis=0, keepdims=True), axis=1, keepdims=True), (8, 128)
+    )
+    total = Total(*total_refs, place, links)
+
+    waiting, active = [total], []
+
+    def beat():
+        for item in list(active):
+            item.beat()
+            if item.stage > 5:
+                active.remove(item)
+        if waiting:
+            item = waiting.pop(0)
+            item.beat()
+            active.append(item)
+
+    def enter(name):
+        for a, b in s.reduce_rows[name]:
+            in_weights = name == "last"
+            waiting.append(
+                Reduce(
+                    b - a,
+                    a + s.down0 if in_weights else a - s.out0,
+                    a,
+                    cut,
+                    W if in_weights else G,
+                    grads_out,
+                    place,
+                    links,
+                    scratch,
+                )
+            )
+
+    def turned(left, right):
+        return lax.dot_general(left, right, (((0,), (0,)), ((), ())), preferred_element_type=f32)
+
+    def by_turned(left, right):
+        return lax.dot_general(left, right, (((1,), (1,)), ((), ())), preferred_element_type=f32)
+
+    def down_grad(t):
+        p, y = t // 2, t % 2
+        cols = pl.ds(pl.multiple_of(y * half, 128), half)
+        value = turned(act[p, :, cols], low2[...]).astype(bf16)
+        G[p, y, :, s.down0 - s.out0 : s.down0 - s.out0 + downs, :] = value.reshape(2, downs, width)
+
+    loop(2 * s.panels, down_grad)
+    enter("down")
+    beat()
+    beat()
+
+    def active_grad(t):
+        p, y = t // 2, t % 2
+        cols = pl.ds(pl.multiple_of(y * half, 128), half)
+        value = by_turned(low2[...], down_block(p, y))
+        gp[p, :, cols] = (value * gp[p, :, cols].astype(f32)).astype(bf16)
+
+    loop(2 * s.panels, active_grad)
+    beat()
+
+    def put_grad(first, m, value):
+        rows = pl.ds(pl.multiple_of(first, 16), shard)
+        return (pl.ds(2 * m, 2), slice(None), slice(None), rows, slice(None)), value.astype(
+            bf16
+        ).reshape(2, 2, 2, shard, width)
+
+    def up_grad(t):
+        m, p = t // s.panels, t % s.panels
+        cols = pl.ds(pl.multiple_of(m * half, 128), half)
+        where, value = put_grad(
+            s.up0 - s.out0 + p * shard, m, turned(low1[:, cols], gp[p])
+        )
+        G[where] = value
+
+    loop(2 * s.panels, up_grad)
+    enter("up")
+    beat()
+
+    def normed_grad(m):
+        cols = pl.ds(pl.multiple_of(m * half, 128), half)
+        value = acc[:, cols]
+        for p in range(s.panels):
+            value = value + by_turned(gp[p], half_rows(s.up0 + p * shard, m))
+        acc[:, cols] = value
+
+    loop(2, normed_grad)
+    beat()
+
+    def first_back(b):
+        rows = pl.ds(pl.multiple_of(b * rows_n, 16), rows_n)
+        grad, normal = acc[rows, :], n1[rows, :]
+        sums[0] += fold(grad * normal)
+        scaled = grad * gains[0:1, :]
+        hidden_grad = r1[rows, 0:1] * (
+            scaled
+            - jnp.mean(scaled, axis=1, keepdims=True)
+            - normal * jnp.mean(scaled * normal, axis=1, keepdims=True)
+        )
+        acc[rows, :] = hidden_grad
+        low2[rows, :] = hidden_grad.astype(bf16)
+
+    loop(span // rows_n, first_back)
+
+    def attn_grad(m):
+        cols = pl.ds(pl.multiple_of(m * half, 128), half)
+        dO[own(0, span), cols] = by_turned(low2[...], half_rows(s.out0, m)).astype(bf16)
+
+    loop(2, attn_grad)
+    head = lax.broadcasted_iota(jnp.int32, (16, width), 0)
+    in_head = jnp.where((feature // HEAD_DIM) == head, 1.0, 0.0)
+
+    def head_delta(b):
+        first = pl.multiple_of(b * 128, 128)
+        rows = pl.ds(first, 128)
+        product = dO[own(first, 128), :].astype(f32) * attn[rows, :].astype(f32)
+        stat[x, 1, :, rows] = lax.dot_general(
+            in_head,
+            product,
+            (((1,), (1,)), ((), ())),
+            precision=lax.Precision.HIGHEST,
+            preferred_element_type=f32,
+        )
+
+    loop(span // 128, head_delta)
+    send_grad = links.start(dO.at[own(0, span)], dO.at[own(0, span)], place.to_x)
+    send_stat = links.start(stat.at[x], stat.at[x], place.to_x)
+
+    def out_grad(m):
+        cols = pl.ds(pl.multiple_of(m * half, 128), half)
+        where, value = put_grad(0, m, turned(attn[:, cols], low2[...]))
+        G[where] = value
+
+    loop(2, out_grad)
+    pieces = []
+    for g in range(2):
+        row = jnp.sum(sums[g], axis=0, keepdims=True)
+        split = jnp.where(mine, jnp.broadcast_to(row, (16, width)), 0.0).astype(bf16)
+        pieces.append(by_turned(split, spread))
+    at_row = lax.broadcasted_iota(jnp.int32, (16, 16, 128), 1)
+    gain_block = jnp.where(
+        at_row == 0, pieces[0][:, None, :], jnp.where(at_row == 1, pieces[1][:, None, :], 0.0)
+    ).astype(bf16)
+    G[:, :, :, shard : shard + 16, :128] = gain_block.reshape(4, 2, 2, 16, 128)
+    G[:, :, :, shard : shard + 16, 128:] = jnp.zeros((4, 2, 2, 16, width - 128), bf16)
+    enter("out")
+    beat()
+
+    rows_k = s.rows_k
+
+    def block_terms(key, value, bias, query, grad, log_row, delta_row):
+        scores = by_turned(key, query) + bias
+        p = jnp.exp(scores - log_row)
+        score_grad = (p * (by_turned(value, grad) - delta_row)).astype(bf16)
+        return p.astype(bf16), score_grad
+
+    def key_bias(rows):
+        column = jnp.where(order_col[rows, :] < length_now, 0.0, MASKED)
+        return jnp.concatenate([column] * (span // 128), axis=1)
+
+    def back_other(pair):
+        lanes = pl.ds(pair * 128, 128)
+
+        def body(b):
+            rows = other(b * rows_k, rows_k)
+            key, value, bias = ks[rows, lanes], vs[rows, lanes], key_bias(rows)
+            query, grad = qs[own(0, span), lanes], dO[own(0, span), lanes]
+            result = jnp.zeros((span, 128), f32)
+            for h, keep in enumerate((even, odd)):
+                at = pl.ds(2 * pair + h, 1)
+                p, score_grad = block_terms(
+                    key, value, bias, query * keep, grad * keep, stat[x, 0, at, :], stat[x, 1, at, :]
+                )
+                result = result + turned(score_grad, key * keep)
+            n1[:, lanes] += result
+
+        n1[:, lanes] = jnp.zeros((span, 128), f32)
+        loop(span // rows_k, body)
+
+    def back_own(pair):
+        lanes = pl.ds(pair * 128, 128)
+
+        def body(b):
+            first = pl.multiple_of(b * rows_k, 16)
+            rows = own(first, rows_k)
+            key, value, bias = ks[rows, lanes], vs[rows, lanes], key_bias(rows)
+            result = jnp.zeros((span, 128), f32)
+            key_grad = jnp.zeros((rows_k, 128), f32)
+            value_grad = jnp.zeros((rows_k, 128), f32)
+            for side in (x, xo):
+                whole = pl.ds(pl.multiple_of(side * span, 16), span)
+                query, grad = qs[whole, lanes], dO[whole, lanes]
+                for h, keep in enumerate((even, odd)):
+                    at = pl.ds(2 * pair + h, 1)
+                    query_h, grad_h = query * keep, grad * keep
+                    p, score_grad = block_terms(
+                        key, value, bias, query_h, grad_h, stat[side, 0, at, :], stat[side, 1, at, :]
+                    )
+                    value_grad = value_grad + dot(p, grad_h)
+                    key_grad = key_grad + dot(score_grad, query_h)
+                    if side is x:
+                        result = result + turned(score_grad, key * keep)
+            out = pl.ds(first, rows_k)
+            n1[:, lanes] += result
+            act[1, out, lanes] = key_grad.astype(bf16)
+            act[2, out, lanes] = value_grad.astype(bf16)
+
+        loop(span // rows_k, body)
+        act[0, :, lanes] = (n1[:, lanes] * SCORE_SCALE).astype(bf16)
+
+    for pair in range(pairs):
+        back_other(pair)
+        if pair in s.beats_other:
+            beat()
+    send_grad.wait_recv()
+    send_stat.wait_recv()
+    for pair in range(pairs):
+        back_own(pair)
+        if pair in s.beats_own:
+            beat()
+
+    def weight_grad(t):
+        j, m = t // 2, t % 2
+        cols = pl.ds(pl.multiple_of(m * half, 128), half)
+        where, value = put_grad(s.down0 + j * shard, m, turned(tok[own(0, span), cols], act[j]))
+        W[where] = value
+
+    loop(6, weight_grad)
+    enter("last")
+    beat()
+
+    def input_grad(m):
+        cols = pl.ds(pl.multiple_of(m * half, 128), half)
+        value = acc[:, cols]
+        for j in range(3):
+            value = value + by_turned(act[j], half_rows(j * shard, m))
+        acc[:, cols] = value
+
+    loop(2, input_grad)
+    token_copy = pltpu.make_async_copy(acc, token_out, local.at[n_gather])
+    token_copy.start()
+    beat()
+    send_result.wait_recv()
+
+    def place_rows(n):
+        cols = pl.ds(pl.multiple_of(n * third, 128), third)
+        value = None
+        position = lax.broadcasted_iota(jnp.int32, (span, s.block), 0) + x * span
+        for c, rows in ((x, teach[x, :, cols]), (xo, res_in[:, cols])):
+            at = order_row[0:1, pl.ds(pl.multiple_of(c * span + x * s.block, 128), s.block)]
+            chosen = jnp.where(position == at, 1.0, 0.0).astype(bf16)
+            part = dot(chosen, rows)
+            value = part if value is None else value + part
+        low2[:, cols] = value.astype(bf16)
+
+    loop(3, place_rows)
+    ordered_copy = pltpu.make_async_copy(low2, ordered_out, local.at[n_gather + 1])
+    ordered_copy.start()
+    while waiting or active:
+        beat()
+    total_out[...] = total.sum()
+    token_copy.wait()
+    ordered_copy.wait()
+    links.drain()
+
+
+class Sizes:
+    def __init__(self, span, width, ff, shard, downs, tokens):
+        self.span, self.width, self.shard, self.downs, self.tokens = span, width, shard, downs, tokens
+        self.panels = ff // width
+        self.block = span // 2
+        self.out0 = 3 * shard
+        self.gain0 = 4 * shard
+        self.up0 = self.gain0 + 16
+        self.down0 = self.up0 + self.panels * shard
+        self.rows = self.down0 + downs
+        self.cut = Cut(width, 2 * (width // 6))
+        self.lag = 1.01
+        up_half = self.up0 + self.panels // 2 * shard
+        up_end = self.down0
+        self.gather_rows = (
+            (0, self.out0),
+            (self.out0, up_half),
+            (up_half, up_end),
+            (up_end, up_end + downs // 2),
+            (up_end + downs // 2, self.rows),
+        )
+        self.up_ready = 2
+        self.reduce_rows = {
+            "down": ((up_end, up_end + downs // 2), (up_end + downs // 2, self.rows)),
+            "up": ((self.up0, up_half), (up_half, up_end)),
+            "out": ((self.out0, self.up0),),
+            "last": ((0, shard), (shard, self.out0)),
+        }
+        self.tick_project, self.tick_attend, self.tick_norm = 1, 2, 1
+        self.rows_q, self.rows_n, self.rows_k = 128, 64, 256
+        self.beats_other, self.beats_own = (1, 3, 5), (0, 1, 2, 3, 4, 5)
+
+
+def layer(s, tokens, packed, teacher, order_row, order_col, length, valid):
+    bf16, f32 = jnp.bfloat16, jnp.float32
+    span, width = s.span, s.width
+    both = 2 * span
+    anywhere = pl.BlockSpec(memory_space=pl.ANY)
+    vmem = pl.BlockSpec(memory_space=pltpu.VMEM)
+    smem = pl.BlockSpec(memory_space=pltpu.SMEM)
+    reduces = sum(len(v) for v in s.reduce_rows.values())
+    copies = (
+        Gather.copies * len(s.gather_rows) + Reduce.copies * reduces + Total.copies + 6
+    )
+    small = pltpu.VMEM((8, 128), f32)
+    scratch = [
+        pltpu.VMEM((4, 2, 2, s.rows, width), bf16),
+        pltpu.VMEM((4, 2, 2, s.rows - s.out0, width), bf16),
+        pltpu.VMEM((both, width), bf16),
+        pltpu.VMEM((both, width), bf16),
+        pltpu.VMEM((both, width), bf16),
+        pltpu.VMEM((both, width), bf16),
+        pltpu.VMEM((both, width), bf16),
+        pltpu.VMEM((2, 2, 16, span), f32),
+        pltpu.VMEM((span, width), bf16),
+        pltpu.VMEM((span, width), f32),
+        pltpu.VMEM((span, 128), f32),
+        pltpu.VMEM((span, width), bf16),
+        pltpu.VMEM((s.panels, span, width), bf16),
+        pltpu.VMEM((s.panels, span, width), bf16),
+        pltpu.VMEM((span, width), f32),
+        pltpu.VMEM((2, s.block, width), bf16),
+        pltpu.VMEM((s.block, width), bf16),
+        pltpu.VMEM((span, width), bf16),
+        pltpu.VMEM((8, width), f32),
+        pltpu.VMEM((3, 8, width), f32),
+        pltpu.VMEM((3, 8, 128), f32),
+        small,
+        small,
+        small,
+        pltpu.VMEM((4, 8, 128), f32),
+        pltpu.SemaphoreType.DMA((copies,)),
+        pltpu.SemaphoreType.DMA((copies,)),
+        pltpu.SemaphoreType.DMA((len(s.gather_rows) + 2,)),
+    ] + reduce_scratch(s.rows, s.cut, width)
+    return pl.pallas_call(
+        functools.partial(layer_kernel, s),
+        out_shape=[
+            jax.ShapeDtypeStruct((span, width), bf16),
+            jax.ShapeDtypeStruct((8, 128), f32),
+            jax.ShapeDtypeStruct((span, width), f32),
+            jax.ShapeDtypeStruct((s.rows, width), bf16),
+        ],
+        in_specs=[anywhere, anywhere, anywhere, vmem, vmem, smem, smem],
+        out_specs=[anywhere, vmem, anywhere, vmem],
+        scratch_shapes=scratch,
+        compiler_params=pltpu.CompilerParams(
+            collective_id=0, has_side_effects=True, vmem_limit_bytes=s.vmem
+        ),
+    )(tokens, packed, teacher, order_row, order_col, length, valid)
+
+
+def fused_shards(
+    tokens,
+    w_query,
+    w_key,
+    w_value,
+    w_out,
+    w_up,
+    w_down,
+    gain_attn,
+    gain_ffn,
+    teacher,
+    seq_lengths,
+    tok_perm,
+    valid_count,
+):
+    f32 = jnp.float32
+    dp_count = lax.axis_size("dp")
+    span, width = tokens.shape[1:]
+    shard, ff = w_up.shape
+    seq_len = tok_perm.shape[1]
+    s = Sizes(span, width, ff, shard, w_down.shape[0], seq_len * dp_count)
+    s.vmem = 63 * MIB
+    gain_rows = jnp.pad(jnp.stack([gain_attn, gain_ffn]), ((0, 14), (0, width - shard)))
+    up_rows = jnp.transpose(w_up.reshape(shard, s.panels, width), (1, 0, 2)).reshape(-1, width)
+    packed = jnp.concatenate([w_query, w_key, w_value, w_out, gain_rows, up_rows, w_down])
+    order = tok_perm[0]
+    ordered, total, token_grad, grads = layer(
+        s,
+        tokens[0],
+        packed,
+        teacher[0],
+        jnp.broadcast_to(order[None, :], (8, seq_len)),
+        jnp.broadcast_to(order[:, None], (seq_len, 128)),
+        seq_lengths,
+        valid_count,
+    )
+    loss = (total[0, 0] / (2.0 * width * valid_count[0].astype(f32))).reshape(1)
+    grads = grads.astype(f32)
+    up = grads[s.up0 : s.down0].reshape(s.panels, shard, width)
+    return (
+        ordered[None],
+        loss,
+        token_grad[None],
+        grads[:shard],
+        grads[shard : 2 * shard],
+        grads[2 * shard : 3 * shard],
+        grads[s.out0 : s.gain0],
+        jnp.transpose(up, (1, 0, 2)).reshape(shard, ff),
+        grads[s.down0 :],
+        grads[s.gain0, :shard],
+        grads[s.gain0 + 1, :shard],
+    )
+
+
 def solution(mesh):
     in_specs = (
         P("dp", "ctx", None),
@@ -347,4 +1322,5 @@
         P("dp"),
         P("dp"),
     )
-    return jax.shard_map(shards, mesh=mesh, in_specs=in_specs, out_specs=out_specs, check_vma=False)
+    body = fused_shards if dict(mesh.shape) == {"dp": 16, "ctx": 2} else shards
+    return jax.shard_map(body, mesh=mesh, in_specs=in_specs, out_specs=out_specs, check_vma=False)

time: 989 us -> 270 us (0.27)
  waiting for transfers between devices: 596 us -> 0 us
  Pallas kernels: 0 us -> 249 us
  matrix products: 138 us -> 0 us
  blocking collectives: 107 us -> 0 us
  local copies, waits for them, and re-layouts: 79.1 us -> 15.3 us
  other arithmetic: 35 us -> 1.98 us
  between operations: 19.2 us -> 3.82 us
    reduce_scatter x5 -> x0, waiting for transfers between devices: 256 us -> none  [the longest x1 78.9 us: shards(): lax.psum_scatter(grad_down_w.astype(jnp.bfloat16), 'dp', scatter_dimensio...]
    pallas_call x0 -> x1, Pallas kernels: none -> 249 us  [layer(): pl.pallas_call(functools.partial(layer_kernel, s), out_shape=[jax.ShapeDt...]
    all_gather x8 -> x0, waiting for transfers between devices: 197 us -> none  [the longest x1 45.6 us: shards(): lax.all_gather(w_down, 'dp', axis=0, tiled=True)]
    dot_general x32 -> x0, matrix products: 138 us -> none  [the longest x6 21.6 us: row_product(): lax.dot_general(left_mat, right_mat, (((0,), (0,)), ((), ())), preferred_...]
    unnamed x20 -> x0, waiting for transfers between devices: 120 us -> none
    unnamed x2 -> x0, blocking collectives: 62 us -> none
    psum x2 -> x0, blocking collectives: 44.6 us -> none  [the longest x1 39.7 us: shards(): total_sq = lax.psum(jnp.sum(residual_err * residual_err), ('dp', 'ctx'))]
    unnamed x84 -> x17, local copies, waits for them, and re-layouts: 30.8 us -> 5.89 us
  transfers between devices with their start and end apart: 19 -> 0, of which waited for: 16 -> 0; matrix products, arithmetic and copies ran while one was open for 14% -> 0% of each run, Pallas kernels for 0% -> 0%
where the time goes in v2:
time: 270 us
  Pallas kernels  249 us (92%)
  local copies, waits for them, and re-layouts  15.3 us (6%)
  between operations  3.82 us (1%)
    pallas_call x1, Pallas kernels, layer(): pl.pallas_call(functools.partial(layer_kernel, s), out_shape=[jax.ShapeDt...  249 us
    unnamed x17, local copies, waits for them, and re-layouts  5.89 us

profile of v2, /device:TPU:0, one launch (start us, length us, event | category | flops | bytes accessed | tf_op | source)
XLA Modules:
  0.0 269.7 jit_solution(11352119935622552289)
XLA Ops:
  0.6 0.0 copy-start.4
  0.7 1.7 broadcast_in_dim.20.refs_4_
  2.4 1.3 broadcast_in_dim.19.refs_3_
  4.3 0.9 constant_dynamic-update-slice_fusion.5
  5.2 0.9 constant_dynamic-update-slice_fusion.4
  6.1 0.9 constant_dynamic-update-slice_fusion.3
  7.0 0.9 constant_dynamic-update-slice_fusion.2
  7.9 0.7 fusion.6
  8.6 1.0 copy.29
  9.6 0.0 copy-done.4
  9.6 0.0 copy-start.2
  10.3 0.3 copy-done.2
  10.6 248.7 %shard_map.212 = (bf16[512,768]{1,0:T(8,128)(2,1)}, f32[8,128]{1,0:T(8,128)}, f32[512,768]{1,0:T(8,128)}, bf16[592,768]{1,0:T(8,128)(2,1)}) custom-call(bf16[512,768]{1,0:T(8,128)(2,1)} %bitcast.30, bf16[592,768]{1,0:T(8,128)(2,1)} %copy-done.2, bf16[512,768]{1,0:T(8,128)(2,1)} %bitcast.31, s32[8,1024]{1,0:T(8,128)} %broadcast_in_dim.19.refs_3_, ...), custom_call_target="tpu_custom_call" | custom-call | tf_op jit(solution)/shard_map/pallas_call | solution.py:1225
  259.2 0.0 copy-start
  259.2 1.9 fusion.8
  261.1 1.3 convert_element_type.10
  262.4 0.0 copy-start.3
  262.4 0.5 slice_bitcast_fusion
  263.0 0.0 copy-done
  263.0 0.9 fusion.7
  263.9 0.0 copy-start.1
  263.9 0.9 copy.27
  264.7 1.2 slice.27
  266.6 0.0 copy-done.3
  266.6 0.9 copy.40
  267.5 0.0 copy-done.1
  267.5 1.1 copy.41
  (2 shorter events, 0.0 us)
Async XLA Ops:
  0.6 9.0 %copy-start.4 = (bf16[192,768]{1,0:T(8,128)(2,1)S(1)}, bf16[192,768]{1,0:T(8,128)(2,1)}, u32[]{:S(2)}) copy-start(bf16[192,768]{1,0:T(8,128)(2,1)} %param.19) | copy-start | bytes 884740
  9.6 0.9 copy-start.2
  259.2 3.7 %copy-start = (bf16[592,768]{1,0:T(8,128)(2,1)S(1)}, bf16[592,768]{1,0:T(8,128)(2,1)}, u32[]{:S(2)}) copy-start(bf16[592,768]{1,0:T(8,128)(2,1)} %get-tuple-element.18) | copy-start | bytes 2727940
  262.4 4.1 %copy-start.3 = (bf16[512,768]{1,0:T(8,128)(2,1)S(1)}, bf16[512,768]{1,0:T(8,128)(2,1)}, u32[]{:S(2)}) copy-start(bf16[512,768]{1,0:T(8,128)(2,1)} %get-tuple-element.15) | copy-start | bytes 2359300
  263.9 3.6 %copy-start.1 = (f32[512,768]{1,0:T(8,128)S(1)}, f32[512,768]{1,0:T(8,128)}, u32[]{:S(2)}) copy-start(f32[512,768]{1,0:T(8,128)} %get-tuple-element.17) | copy-start | bytes 4718596

commit v3 on v2

--- a/solution.py
+++ b/solution.py
@@ -16,6 +16,12 @@
 MASKED = -1e30
 MESH = pl.DeviceIdType.MESH
 MIB = 1024 * 1024
+
+
+GATHER_SPLIT = (3, 4, 5, 6, 7, 8, 9)
+EARLY = 3
+FORWARD = ((0, 1, 2, 3, 4, 5, 6, 7, 8, 9, 10, 11), (), (0, 0, 0, 1, 2, 1, 1, 3, 2, 2), (3, 4, 5), (6,), (3, 4, 7, 3), (5, 6, 8, 9), (4, 7, 10, 4), (5,), (5, 6, 8, 10, 9, 6, 11), (7, 10), (), (7, 8), (8, 11), (), (9, 11), (), (), (), (9,), (), (), (), (), (), (), (), (), (), ())
+BACKWARD = ((0, 1), (0, 2), (1, 3), (2, 4), (3,), (0, 4, 5), (1,), (5, 6), (), (7,), (2, 6, 7, 1), (8,), (0, 1, 3, 8), (0, 2), (4, 9), (2, 3), (9, 5), (), (4,), (), (6,), (3, 4, 5, 6, 7, 8), (5, 6, 10), (9, 7, 10), (7, 11), (8, 11, 10), (8, 9, 12), (11, 12, 9), (10,), (10, 11, 12, 11, 12, 12))
 
 
 def gelu_exact(values):
@@ -369,32 +375,34 @@
     def drain(self):
         for copy in self.all:
             copy.wait_send()
-
-
-class Cut:
-    def __init__(self, width, first):
-        self.full = width // 2
-        self.one, self.two = first, width // 2 - first
-
-    def half(self, x):
-        return pl.ds(pl.multiple_of(x * self.full, 128), self.full)
-
-    def first(self, x):
-        return pl.ds(pl.multiple_of(x * self.full, 128), self.one)
-
-    def second(self, x):
-        return pl.ds(pl.multiple_of(x * self.full + self.one, 128), self.two)
+        self.all = []
 
 
 class Gather:
-    copies = 23
-
-    def __init__(self, rows, cut, shard, whole, place, links, own_sem):
-        self.rows, self.cut, self.shard, self.whole = rows, cut, shard, whole
+    copies = 20
+
+    def __init__(self, block, early, shard, whole, place, links, own_sem):
+        first, last, self.split = block[:3]
+        self.early = early
+        self.rows = pl.ds(first, last - first)
+        self.width = block[3] if len(block) > 3 else whole.shape[-1]
+        self.shard, self.whole = shard, whole
         self.p, self.links = place, links
         self.own = pltpu.make_async_copy(
-            shard.at[rows], whole.at[place.z, place.y, place.c, rows], own_sem
-        )
+            shard.at[self.rows, self.cols()],
+            whole.at[place.z, place.y, place.c, self.rows, self.cols()],
+            own_sem,
+        )
+        self.last = 4 if self.split else 3
+
+    def cols(self):
+        return pl.ds(0, self.width)
+
+    def half(self, x):
+        if not self.split:
+            return self.cols()
+        size = self.width // 2
+        return pl.ds(pl.multiple_of(x * size, 128), size)
 
     def piece(self, z, y, cols):
         return self.whole.at[z, y, self.p.c, self.rows, cols]
@@ -403,62 +411,97 @@
         return self.links.start(piece, piece, partner)
 
     def step0(self):
-        p, rows = self.p, self.rows
-        mine = self.cut.half(p.x)
-        source, target = self.shard.at[rows, mine], self.piece(p.z, p.y, mine)
+        p = self.p
+        mine = self.half(p.x)
+        source, target = self.shard.at[self.rows, mine], self.piece(p.z, p.y, mine)
         self.from_z = [self.links.start(source, target, p.to_z[k]) for k in range(1, 4)]
         self.own.start()
-        self.from_y = [self.links.start(source, target, p.to_y)]
+        if self.early:
+            self.spread()
+
+    def spread(self):
+        p = self.p
+        mine = self.half(p.x)
+        self.from_y = [
+            self.links.start(self.shard.at[self.rows, mine], self.piece(p.z, p.y, mine), p.to_y)
+        ]
         self.from_c = [
-            self.links.start(self.shard.at[rows], self.whole.at[p.z, p.y, p.c, rows], p.to_c)
+            self.links.start(
+                self.shard.at[self.rows, self.cols()], self.piece(p.z, p.y, self.cols()), p.to_c
+            )
         ]
 
     def step1(self):
         p = self.p
+        if not self.early:
+            self.spread()
         self.from_x = []
         for k in range(1, 4):
             self.from_z[k - 1].wait_recv()
-            piece = self.piece(p.z_down[k], p.y, self.cut.half(p.x))
-            self.from_x.append(self.push(piece, p.to_x))
+            piece = self.piece(p.z_down[k], p.y, self.half(p.x))
             self.from_y.append(self.push(piece, p.to_y))
+            if self.split:
+                self.from_x.append(self.push(piece, p.to_x))
             self.from_c.append(self.push(piece, p.to_c))
 
     def step2(self):
-        p, cut, every = self.p, self.cut, slice(None)
-        self.own.wait()
-        for k in range(1, 4):
-            self.from_x[k - 1].wait_recv()
-        self.first_y = self.push(self.piece(every, p.y, cut.first(p.xo)), p.to_y)
-        for k in range(1, 4):
-            self.from_c.append(self.push(self.piece(p.z_down[k], p.y, cut.half(p.xo)), p.to_c))
+        p, every = self.p, slice(None)
         for copy in self.from_y:
             copy.wait_recv()
-        self.second_x = self.push(self.piece(every, p.yo, cut.second(p.x)), p.to_x)
-        self.from_c.append(self.push(self.piece(every, p.yo, cut.half(p.x)), p.to_c))
+        piece = self.piece(every, p.yo, self.half(p.x))
+        if self.split:
+            self.across = self.push(piece, p.to_x)
+        self.from_c.append(self.push(piece, p.to_c))
+        for k, copy in enumerate(self.from_x):
+            copy.wait_recv()
+            piece = self.piece(p.z_down[k + 1], p.y, self.half(p.xo))
+            self.from_c.append(self.push(piece, p.to_c))
 
     def step3(self):
-        p, cut, every = self.p, self.cut, slice(None)
-        self.first_y.wait_recv()
-        self.from_c.append(self.push(self.piece(every, p.yo, cut.first(p.xo)), p.to_c))
-        self.second_x.wait_recv()
-        self.from_c.append(self.push(self.piece(every, p.yo, cut.second(p.xo)), p.to_c))
+        if self.split:
+            self.across.wait_recv()
+            piece = self.piece(slice(None), self.p.yo, self.half(self.p.xo))
+            self.from_c.append(self.push(piece, self.p.to_c))
+        else:
+            self.step4()
 
     def step4(self):
         for copy in self.from_c:
             copy.wait_recv()
+        self.own.wait()
 
 
 class Reduce:
-    copies = 10
-
-    def __init__(self, rows, at, first_row, cut, grads, out, place, links, scratch):
-        self.rows, self.cut, self.grads, self.out = rows, cut, grads, out
-        self.at, self.here = pl.ds(at, rows), pl.ds(first_row, rows)
-        self.at0, self.here0 = at, first_row
+    copies = 7
+
+    def __init__(self, block, at, grads, out, place, links, core_in, bufs):
+        first, last, self.split = block[:3]
+        self.col0, self.width = (0, grads.shape[-1]) if len(block) < 4 else block[3]
+        self.rows = last - first
+        self.at0, self.here0 = at, first
+        self.at, self.here = pl.ds(at, self.rows), pl.ds(first, self.rows)
+        self.grads, self.out = grads, out
         self.p, self.links = place, links
-        self.core_in, self.x_in, self.y_in, self.y_in2, self.x_in2, self.z_in = scratch
-        self.block = max(b for b in range(16, min(rows, 96) + 1, 16) if rows % b == 0)
+        self.core_in, self.bufs = core_in, bufs
+        limit = max(48, 96 * 768 // self.width)
+        self.block = max(b for b in range(16, min(self.rows, limit) + 1, 16) if self.rows % b == 0)
         self.stage = 0
+        self.last = 5 if self.split else 4
+
+    def cols(self):
+        return pl.ds(self.col0, self.width)
+
+    def half(self, x):
+        if not self.split:
+            return self.cols()
+        size = self.width // 2
+        return pl.ds(pl.multiple_of(self.col0 + x * size, 128), size)
+
+    def low(self):
+        return pl.ds(self.col0, self.width // 2)
+
+    def high(self):
+        return pl.ds(self.col0 + self.width // 2, self.width // 2) if self.split else self.cols()
 
     def add(self, outer, target, source):
         steps = self.rows // self.block
@@ -477,114 +520,146 @@
     def step0(self):
         p = self.p
         self.by_core = self.links.start(
-            self.grads.at[:, :, p.co, self.at], self.core_in.at[:, :, self.here], p.to_c
-        )
-
-    def step1(self):
-        p, cut, grads = self.p, self.cut, self.grads
-        self.by_core.wait_recv()
-        self.add(
-            8,
-            lambda i, rows: (i // 2, i % 2, p.c, rows),
-            lambda i, rows: self.core_in[i // 2, i % 2, rows],
-        )
-        self.by_y = [
-            self.links.start(
-                grads.at[:, p.yo, p.c, self.at, cut.first(h)], self.y_in.at[h, :, self.here], p.to_y
-            )
-            for h in range(2)
-        ]
-        self.by_x = self.links.start(
-            grads.at[:, :, p.c, self.at, cut.second(p.xo)], self.x_in.at[:, :, self.here], p.to_x
-        )
-
-    def step2(self):
-        p, cut, grads = self.p, self.cut, self.grads
-        for h in range(2):
-            self.by_y[h].wait_recv()
-            self.add(
-                4,
-                lambda i, rows: (i, p.y, p.c, rows, cut.first(h)),
-                lambda i, rows: self.y_in[h, i, rows],
-            )
-        self.by_x2 = self.links.start(
-            grads.at[:, p.y, p.c, self.at, cut.first(p.xo)], self.x_in2.at[:, self.here], p.to_x
-        )
-        self.by_x.wait_recv()
-        self.add(
-            8,
-            lambda i, rows: (i // 2, i % 2, p.c, rows, cut.second(p.x)),
-            lambda i, rows: self.x_in[i // 2, i % 2, rows],
-        )
-        self.by_y2 = self.links.start(
-            grads.at[:, p.yo, p.c, self.at, cut.second(p.x)], self.y_in2.at[:, self.here], p.to_y
-        )
-
-    def step3(self):
-        p, cut, grads = self.p, self.cut, self.grads
-        self.by_x2.wait_recv()
+            self.grads.at[:, :, p.co, self.at, self.cols()],
+            self.core_in.at[:, :, self.here, self.cols()],
+            p.to_c,
+        )
+
+    def add_core(self, y):
+        p = self.p
         self.add(
             4,
-            lambda i, rows: (i, p.y, p.c, rows, cut.first(p.x)),
-            lambda i, rows: self.x_in2[i, rows],
-        )
-        self.by_y2.wait_recv()
+            lambda i, rows: (i, y, p.c, rows, self.cols()),
+            lambda i, rows: self.core_in[i, y, rows, self.cols()],
+        )
+
+    def send_y(self):
+        p = self.p
+        self.by_y = self.links.start(
+            self.grads.at[:, p.yo, p.c, self.at, self.half(p.x)],
+            self.bufs.at[pl.ds(0, 4), self.here, self.high()],
+            p.to_y,
+        )
+
+    def step1(self):
+        p = self.p
+        self.by_core.wait_recv()
+        self.add_core(p.yo)
+        if not self.split:
+            self.send_y()
+        self.add_core(p.y)
+        if self.split:
+            self.by_x = [
+                self.links.start(
+                    self.grads.at[:, y, p.c, self.at, self.half(p.xo)],
+                    self.bufs.at[pl.ds(4 * i, 4), self.here, self.low()],
+                    p.to_x,
+                )
+                for i, y in enumerate((p.yo, p.y))
+            ]
+
+    def add_x(self, i, y):
+        p = self.p
+        self.by_x[i].wait_recv()
         self.add(
             4,
-            lambda i, rows: (i, p.y, p.c, rows, cut.second(p.x)),
-            lambda i, rows: self.y_in2[i, rows],
+            lambda j, rows: (j, y, p.c, rows, self.half(p.x)),
+            lambda j, rows: self.bufs[4 * i + j, rows, self.low()],
+        )
+
+    def step2(self):
+        if self.split:
+            self.add_x(0, self.p.yo)
+            self.send_y()
+            self.add_x(1, self.p.y)
+        else:
+            self.reduce_y()
+
+    def reduce_y(self):
+        p = self.p
+        self.by_y.wait_recv()
+        self.add(
+            4,
+            lambda i, rows: (i, p.y, p.c, rows, self.half(p.x)),
+            lambda i, rows: self.bufs[i, rows, self.high()],
         )
         self.by_z = [
             self.links.start(
-                grads.at[p.z_up[k], p.y, p.c, self.at, cut.half(p.x)],
-                self.z_in.at[k - 1, self.here],
+                self.grads.at[p.z_up[k], p.y, p.c, self.at, self.half(p.x)],
+                self.bufs.at[3 + k, self.here, self.high()],
                 p.to_z[k],
             )
             for k in range(1, 4)
         ]
 
-    def step4(self):
-        p, mine = self.p, self.cut.half(self.p.x)
+    def reduce_z(self, put):
+        p = self.p
         for copy in self.by_z:
             copy.wait_recv()
 
         def body(i, carry):
             first = pl.multiple_of(i * self.block, 16)
             rows = pl.ds(self.here0 + first, self.block)
-            total = self.grads[p.z, p.y, p.c, pl.ds(self.at0 + first, self.block), mine].astype(
-                jnp.float32
-            )
+            place = (p.z, p.y, p.c, pl.ds(self.at0 + first, self.block), self.half(p.x))
+            total = self.grads[place].astype(jnp.float32)
             for k in range(3):
-                total = total + self.z_in[k, rows].astype(jnp.float32)
-            self.out[rows, mine] = total.astype(jnp.bfloat16)
+                total = total + self.bufs[4 + k, rows, self.high()].astype(jnp.float32)
+            put(rows, place, total.astype(jnp.bfloat16))
             return carry
 
         lax.fori_loop(0, self.rows // self.block, body, 0)
-        done = self.out.at[self.here, mine]
-        self.last = self.links.start(done, done, p.to_x)
+
+    def step3(self):
+        p = self.p
+        if self.split:
+            self.reduce_y()
+            return
+
+        def put(rows, place, value):
+            self.grads[place] = value
+
+        self.reduce_z(put)
+        self.by_x = self.links.start(
+            self.grads.at[p.z, p.y, p.c, self.at, self.cols()],
+            self.bufs.at[7, self.here, self.cols()],
+            p.to_x,
+        )
+
+    def step4(self):
+        p = self.p
+        if self.split:
+
+            def put(rows, place, value):
+                self.out[rows, self.half(p.x)] = value
+
+            self.reduce_z(put)
+            done = self.out.at[self.here, self.half(p.x)]
+            self.by_x = self.links.start(done, done, p.to_x)
+            return
+        self.by_x.wait_recv()
+
+        def body(i, carry):
+            first = pl.multiple_of(i * self.block, 16)
+            rows = pl.ds(self.here0 + first, self.block)
+            own = self.grads[p.z, p.y, p.c, pl.ds(self.at0 + first, self.block), self.cols()]
+            self.out[rows, self.cols()] = (
+                own.astype(jnp.float32) + self.bufs[7, rows, self.cols()].astype(jnp.float32)
+            ).astype(jnp.bfloat16)
+            return carry
+
+        lax.fori_loop(0, self.rows // self.block, body, 0)
 
     def step5(self):
-        self.last.wait_recv()
+        self.by_x.wait_recv()
 
     def beat(self):
         getattr(self, "step" + str(self.stage))()
         self.stage += 1
 
 
-def reduce_scratch(rows, cut, width):
-    bf16 = jnp.bfloat16
-    return [
-        pltpu.VMEM((4, 2, rows, width), bf16),
-        pltpu.VMEM((4, 2, rows, cut.two), bf16),
-        pltpu.VMEM((2, 4, rows, cut.one), bf16),
-        pltpu.VMEM((4, rows, cut.two), bf16),
-        pltpu.VMEM((4, rows, cut.one), bf16),
-        pltpu.VMEM((3, rows, cut.full), bf16),
-    ]
-
-
 class Total:
     copies = 6
+    last = 4
 
     def __init__(self, value, core_in, x_in, y_in, by_z, place, links):
         self.value, self.core_in, self.x_in, self.y_in, self.by_z = value, core_in, x_in, y_in, by_z
@@ -616,9 +691,6 @@
         for copy in self.spread:
             copy.wait_recv()
 
-    def step5(self):
-        pass
-
     def sum(self):
         return ((self.by_z[0] + self.by_z[1]) + self.by_z[2]) + self.by_z[3]
 
@@ -636,10 +708,10 @@
 
 
 def layer_kernel(s, *refs):
-    (tokens, packed, teacher, order_row, order_col, length, valid) = refs[:7]
-    (ordered_out, total_out, token_out, grads_out) = refs[7:11]
-    (W, G, tok, qs, ks, vs, dO, stat, attn, n1, r1, low1, act, gp, acc, teach, res_in, low2, gains, sums) = refs[11:31]
-    total_refs, (send, recv, local), scratch = refs[31:36], refs[36:39], refs[39:]
+    (tokens, packed, teacher, order_row, length, valid) = refs[:6]
+    (ordered_out, total_out, token_out, grads_out) = refs[6:10]
+    (W, G, tok, qs, ks, vs, dO, stat, attn, n1, r1, low1, act, gp, acc, teach, res_in, low2, gains, sums) = refs[10:30]
+    total_refs, (send, recv, local), (order_col, core_in, bufs) = refs[30:35], refs[35:38], refs[38:]
     f32, bf16 = jnp.float32, jnp.bfloat16
     span, width, shard, downs = s.span, s.width, s.shard, s.downs
     pairs = width // 128
@@ -647,7 +719,6 @@
     half = width // 2
     place = Place()
     x, xo = place.x, place.xo
-    cut = s.cut
     links = Links(send, recv)
 
     def own(first, size):
@@ -672,42 +743,40 @@
         rows = pl.ds(pl.multiple_of(first, 16), shard)
         return W[pl.ds(2 * m, 2), :, :, rows, :].reshape(half, width)
 
-    def down_block(p, y):
-        return W[p, y, :, s.down0 : s.down0 + downs, :].reshape(2 * downs, width)
-
     gathers = [
-        Gather(pl.ds(a, b - a), cut, packed, W, place, links, local.at[i])
-        for i, (a, b) in enumerate(s.gather_rows)
+        Gather(block, i < s.early, packed, W, place, links, local.at[i])
+        for i, block in enumerate(s.gather_blocks)
     ]
     n_gather = len(gathers)
-    order = sorted(
-        [(step + s.lag * i, i, step) for i in range(n_gather) for step in range(5)]
-    )
-    ready = [order.index(entry) for entry in order if entry[2] == 4]
-    done = [0]
-
-    def run_until(index):
-        while done[0] <= index:
-            entry = order[done[0]]
-            getattr(gathers[entry[1]], "step" + str(entry[2]))()
-            done[0] += 1
-
-    def tick(count):
-        run_until(min(done[0] + count, len(order)) - 1)
+    stages = [0] * n_gather
+    forward = iter(s.forward)
+
+    def advance():
+        for i in next(forward):
+            getattr(gathers[i], "step" + str(stages[i]))()
+            stages[i] += 1
+
+    def arrived(first, last):
+        advance()
+        for i, block in enumerate(s.gather_blocks):
+            if block[0] < last and block[1] > first:
+                assert stages[i] > gathers[i].last
 
     place.barrier()
     own_tokens = pltpu.make_async_copy(tokens, tok.at[own(0, span)], local.at[n_gather])
     own_tokens.start()
     own_teacher = pltpu.make_async_copy(teacher, gp.at[0], local.at[n_gather + 1])
     own_teacher.start()
-    run_until(0)
     send_tokens = links.start(tokens, tok.at[own(0, span)], place.to_x)
+    advance()
+    order_col[...] = jnp.broadcast_to(order_row[...].astype(f32), (128, 2 * span)).T
     length_now = length[0]
+    length_float = length_now.astype(f32)
     iota_rows = lax.broadcasted_iota(jnp.int32, (s.block, span), 1)
 
     def pick(c):
         rows = pl.ds(pl.multiple_of(c * span + x * s.block, 16), s.block)
-        position = order_col[rows, :] - x * span
+        position = order_col[rows, :].astype(jnp.int32) - x * span
         chosen = iota_rows == jnp.concatenate([position] * (span // 128), axis=1)
         return jnp.where(chosen, 1.0, 0.0).astype(bf16)
 
@@ -716,8 +785,9 @@
         cols = slice(n * third, (n + 1) * third)
         gp[1, : s.block, cols] = dot(pick(xo), gp[0, :, cols]).astype(bf16)
         teach[x, :, cols] = dot(pick(x), gp[0, :, cols]).astype(bf16)
-    run_until(ready[0])
     teach_copy = links.start(gp.at[1, pl.ds(0, s.block)], teach.at[x], place.to_x)
+    advance()
+    arrived(0, s.out0)
 
     own_tokens.wait()
 
@@ -732,10 +802,10 @@
 
     sets = ((0, qs, SCORE_SCALE), (shard, ks, 1.0), (2 * shard, vs, 1.0))
     project(own(0, span), sets)
-    tick(s.tick_project)
+    advance()
     send_tokens.wait_recv()
     project(other(0, span), sets)
-    tick(s.tick_project)
+    advance()
 
     lane = lax.broadcasted_iota(jnp.int32, (1, 128), 1)
     even32 = lane < HEAD_DIM
@@ -777,9 +847,9 @@
 
     for pair in range(pairs):
         attend(pair)
-        tick(s.tick_attend)
-
-    run_until(ready[1])
+        advance()
+
+    arrived(s.out0, s.up0)
     device = lax.broadcasted_iota(jnp.int32, (16, width), 0)
     feature = lax.broadcasted_iota(jnp.int32, (16, width), 1)
     mine = (feature // shard) == device
@@ -799,6 +869,7 @@
         acc[:, cols] = dot(attn[...], by_columns(s.out0, n))
 
     loop(3, branch)
+    advance()
     rows_n = s.rows_n
 
     def wide_column(column):
@@ -816,33 +887,36 @@
         low1[rows, :] = (normal * gains[0:1, :]).astype(bf16)
 
     loop(span // rows_n, first_norm)
-    tick(s.tick_norm)
+    advance()
 
     teach_copy.wait_recv()
     links.sent(teach_copy)
-    run_until(ready[s.up_ready])
-
-    def upward(t):
-        p, n = t // 3, t % 3
-        cols = pl.ds(pl.multiple_of(n * third, 128), third)
-        value = dot(low1[...], by_columns(s.up0 + p * shard, n))
-        cdf = 0.5 * (1.0 + lax.erf(value * ROOT_HALF))
-        act[p, :, cols] = (value * cdf).astype(bf16)
-        gp[p, :, cols] = (cdf + value * (jnp.exp(-0.5 * value * value) * DENSITY)).astype(bf16)
-
-    loop(3 * s.panels, upward)
-    run_until(len(order) - 1)
-
-    def downward(n):
-        cols = pl.ds(pl.multiple_of(n * third, 128), third)
-        value = None
-        for p in range(s.panels):
-            weight = W[p, :, :, s.down0 : s.down0 + downs, cols].reshape(width, third)
-            part = dot(act[p], weight)
-            value = part if value is None else value + part
-        acc[:, cols] = value
-
-    loop(3, downward)
+
+    def upward(p):
+        def body(n):
+            cols = pl.ds(pl.multiple_of(n * third, 128), third)
+            value = dot(low1[...], by_columns(s.up0 + p * shard, n))
+            cdf = 0.5 * (1.0 + lax.erf(value * ROOT_HALF))
+            act[p, :, cols] = (value * cdf).astype(bf16)
+            gp[p, :, cols] = (cdf + value * (jnp.exp(-0.5 * value * value) * DENSITY)).astype(bf16)
+
+        loop(3, body)
+
+    def downward(p):
+        def body(n):
+            cols = pl.ds(pl.multiple_of(n * third, 128), third)
+            value = dot(act[p], by_columns(s.down0 + p * shard, n))
+            acc[:, cols] = value if p == 0 else acc[:, cols] + value
+
+        loop(3, body)
+
+    for p in range(s.panels):
+        arrived(s.up0 + p * shard, s.up0 + (p + 1) * shard)
+        upward(p)
+        advance()
+        arrived(s.down0 + p * shard, s.down0 + (p + 1) * shard)
+        downward(p)
+        advance()
 
     sums[...] = jnp.zeros_like(sums)
     valid_total = jnp.full((1, 1), valid[0], jnp.int32).astype(f32)
@@ -864,7 +938,7 @@
         at = pl.ds(pl.multiple_of((b % per) * rows_n, 16), rows_n)
         target = teach[b // per, at, :].astype(f32)
         teach[b // per, at, :] = result
-        live = order_col[own(first, rows_n), 0:1] < length_now
+        live = order_col[own(first, rows_n), 0:1] < length_float
         error = jnp.where(live, result.astype(f32) - target, 0.0)
         sums[2] += fold(error * error)
         grad = (error * grad_scale).astype(bf16).astype(f32)
@@ -880,67 +954,39 @@
 
     loop(span // rows_n, second_norm)
     links.drain()
-    links.all = []
     send_result = links.start(teach.at[xo], res_in, place.to_x)
     total_refs[0][0] = jnp.broadcast_to(
         jnp.sum(jnp.sum(sums[2], axis=0, keepdims=True), axis=1, keepdims=True), (8, 128)
     )
     total = Total(*total_refs, place, links)
 
-    waiting, active = [total], []
+    reduces = [total]
+    backward = iter(s.backward)
 
     def beat():
-        for item in list(active):
-            item.beat()
-            if item.stage > 5:
-                active.remove(item)
-        if waiting:
-            item = waiting.pop(0)
-            item.beat()
-            active.append(item)
-
-    def enter(name):
-        for a, b in s.reduce_rows[name]:
-            in_weights = name == "last"
-            waiting.append(
-                Reduce(
-                    b - a,
-                    a + s.down0 if in_weights else a - s.out0,
-                    a,
-                    cut,
-                    W if in_weights else G,
-                    grads_out,
-                    place,
-                    links,
-                    scratch,
-                )
+        for i in next(backward):
+            reduces[i].beat()
+
+    def enter(block, in_weights=False):
+        first = block[0]
+        reduces.append(
+            Reduce(
+                block,
+                first + s.down0 if in_weights else first - s.out0,
+                W if in_weights else G,
+                grads_out,
+                place,
+                links,
+                core_in,
+                bufs,
             )
+        )
 
     def turned(left, right):
         return lax.dot_general(left, right, (((0,), (0,)), ((), ())), preferred_element_type=f32)
 
     def by_turned(left, right):
         return lax.dot_general(left, right, (((1,), (1,)), ((), ())), preferred_element_type=f32)
-
-    def down_grad(t):
-        p, y = t // 2, t % 2
-        cols = pl.ds(pl.multiple_of(y * half, 128), half)
-        value = turned(act[p, :, cols], low2[...]).astype(bf16)
-        G[p, y, :, s.down0 - s.out0 : s.down0 - s.out0 + downs, :] = value.reshape(2, downs, width)
-
-    loop(2 * s.panels, down_grad)
-    enter("down")
-    beat()
-    beat()
-
-    def active_grad(t):
-        p, y = t // 2, t % 2
-        cols = pl.ds(pl.multiple_of(y * half, 128), half)
-        value = by_turned(low2[...], down_block(p, y))
-        gp[p, :, cols] = (value * gp[p, :, cols].astype(f32)).astype(bf16)
-
-    loop(2 * s.panels, active_grad)
-    beat()
 
     def put_grad(first, m, value):
         rows = pl.ds(pl.multiple_of(first, 16), shard)
@@ -948,17 +994,33 @@
             bf16
         ).reshape(2, 2, 2, shard, width)
 
-    def up_grad(t):
-        m, p = t // s.panels, t % s.panels
-        cols = pl.ds(pl.multiple_of(m * half, 128), half)
-        where, value = put_grad(
-            s.up0 - s.out0 + p * shard, m, turned(low1[:, cols], gp[p])
-        )
-        G[where] = value
-
-    loop(2 * s.panels, up_grad)
-    enter("up")
-    beat()
+    def panel_grad(first, left, right):
+        def body(m):
+            cols = pl.ds(pl.multiple_of(m * half, 128), half)
+            where, value = put_grad(first - s.out0, m, turned(left[:, cols], right[...]))
+            G[where] = value
+
+        loop(2, body)
+
+    for p in range(s.panels):
+        panel_grad(s.down0 + p * shard, act.at[p], low2)
+        enter(s.down_blocks[p])
+        beat()
+
+    def active_grad(p):
+        def body(m):
+            cols = pl.ds(pl.multiple_of(m * half, 128), half)
+            value = by_turned(low2[...], half_rows(s.down0 + p * shard, m))
+            gp[p, :, cols] = (value * gp[p, :, cols].astype(f32)).astype(bf16)
+
+        loop(2, body)
+
+    for p in range(s.panels):
+        active_grad(p)
+        beat()
+        panel_grad(s.up0 + p * shard, low1, gp.at[p])
+        enter(s.up_blocks[p])
+        beat()
 
     def normed_grad(m):
         cols = pl.ds(pl.multiple_of(m * half, 128), half)
@@ -984,6 +1046,7 @@
         low2[rows, :] = hidden_grad.astype(bf16)
 
     loop(span // rows_n, first_back)
+    beat()
 
     def attn_grad(m):
         cols = pl.ds(pl.multiple_of(m * half, 128), half)
@@ -1009,12 +1072,7 @@
     send_grad = links.start(dO.at[own(0, span)], dO.at[own(0, span)], place.to_x)
     send_stat = links.start(stat.at[x], stat.at[x], place.to_x)
 
-    def out_grad(m):
-        cols = pl.ds(pl.multiple_of(m * half, 128), half)
-        where, value = put_grad(0, m, turned(attn[:, cols], low2[...]))
-        G[where] = value
-
-    loop(2, out_grad)
+    panel_grad(s.out0, attn, low2)
     pieces = []
     for g in range(2):
         row = jnp.sum(sums[g], axis=0, keepdims=True)
@@ -1026,7 +1084,7 @@
     ).astype(bf16)
     G[:, :, :, shard : shard + 16, :128] = gain_block.reshape(4, 2, 2, 16, 128)
     G[:, :, :, shard : shard + 16, 128:] = jnp.zeros((4, 2, 2, 16, width - 128), bf16)
-    enter("out")
+    enter(s.out_block)
     beat()
 
     rows_k = s.rows_k
@@ -1038,7 +1096,7 @@
         return p.astype(bf16), score_grad
 
     def key_bias(rows):
-        column = jnp.where(order_col[rows, :] < length_now, 0.0, MASKED)
+        column = jnp.where(order_col[rows, :] < length_float, 0.0, MASKED)
         return jnp.concatenate([column] * (span // 128), axis=1)
 
     def back_other(pair):
@@ -1091,26 +1149,28 @@
         loop(span // rows_k, body)
         act[0, :, lanes] = (n1[:, lanes] * SCORE_SCALE).astype(bf16)
 
+    def weight_grad(j, columns):
+        def body(m):
+            cols = pl.ds(pl.multiple_of(m * half, 128), half)
+            value = turned(tok[own(0, span), cols], act[j, :, columns]).astype(bf16)
+            W[
+                pl.ds(2 * m, 2), :, :, s.down0 + j * shard : s.down0 + (j + 1) * shard, columns
+            ] = value.reshape(2, 2, 2, shard, 256)
+
+        loop(2, body)
+
     for pair in range(pairs):
         back_other(pair)
-        if pair in s.beats_other:
-            beat()
+        beat()
     send_grad.wait_recv()
     send_stat.wait_recv()
     for pair in range(pairs):
         back_own(pair)
-        if pair in s.beats_own:
-            beat()
-
-    def weight_grad(t):
-        j, m = t // 2, t % 2
-        cols = pl.ds(pl.multiple_of(m * half, 128), half)
-        where, value = put_grad(s.down0 + j * shard, m, turned(tok[own(0, span), cols], act[j]))
-        W[where] = value
-
-    loop(6, weight_grad)
-    enter("last")
-    beat()
+        if pair % 2 == 1:
+            for j in range(3):
+                weight_grad(j, slice((pair - 1) * 128, (pair + 1) * 128))
+            enter(s.last_blocks[pair // 2], True)
+        beat()
 
     def input_grad(m):
         cols = pl.ds(pl.multiple_of(m * half, 128), half)
@@ -1139,8 +1199,9 @@
     loop(3, place_rows)
     ordered_copy = pltpu.make_async_copy(low2, ordered_out, local.at[n_gather + 1])
     ordered_copy.start()
-    while waiting or active:
-        beat()
+    beat()
+    beat()
+    assert all(item.stage > item.last for item in reduces)
     total_out[...] = total.sum()
     token_copy.wait()
     ordered_copy.wait()
@@ -1157,40 +1218,30 @@
         self.up0 = self.gain0 + 16
         self.down0 = self.up0 + self.panels * shard
         self.rows = self.down0 + downs
-        self.cut = Cut(width, 2 * (width // 6))
-        self.lag = 1.01
-        up_half = self.up0 + self.panels // 2 * shard
-        up_end = self.down0
-        self.gather_rows = (
-            (0, self.out0),
-            (self.out0, up_half),
-            (up_half, up_end),
-            (up_end, up_end + downs // 2),
-            (up_end + downs // 2, self.rows),
-        )
-        self.up_ready = 2
-        self.reduce_rows = {
-            "down": ((up_end, up_end + downs // 2), (up_end + downs // 2, self.rows)),
-            "up": ((self.up0, up_half), (up_half, up_end)),
-            "out": ((self.out0, self.up0),),
-            "last": ((0, shard), (shard, self.out0)),
-        }
-        self.tick_project, self.tick_attend, self.tick_norm = 1, 2, 1
+        panels = [self.up0 + p * shard for p in range(self.panels)]
+        lower = [self.down0 + p * shard for p in range(self.panels)]
+        blocks = [(j * shard, (j + 1) * shard) for j in range(3)] + [(self.out0, self.up0)]
+        for up, down in zip(panels, lower):
+            blocks += [(up, up + shard), (down, down + shard)]
+        self.gather_blocks = tuple(b + (i in GATHER_SPLIT,) for i, b in enumerate(blocks))
+        self.early = EARLY
+        self.up_blocks = [(up, up + shard, False) for up in panels]
+        self.down_blocks = [(down, down + shard, False) for down in lower]
+        self.out_block = (self.out0, self.up0, False)
+        self.last_blocks = [(0, self.out0, False, (256 * j, 256)) for j in range(width // 256)]
+        self.forward, self.backward = FORWARD, BACKWARD
         self.rows_q, self.rows_n, self.rows_k = 128, 64, 256
-        self.beats_other, self.beats_own = (1, 3, 5), (0, 1, 2, 3, 4, 5)
-
-
-def layer(s, tokens, packed, teacher, order_row, order_col, length, valid):
+
+
+def layer(s, tokens, packed, teacher, order_row, length, valid):
     bf16, f32 = jnp.bfloat16, jnp.float32
     span, width = s.span, s.width
     both = 2 * span
     anywhere = pl.BlockSpec(memory_space=pl.ANY)
     vmem = pl.BlockSpec(memory_space=pltpu.VMEM)
     smem = pl.BlockSpec(memory_space=pltpu.SMEM)
-    reduces = sum(len(v) for v in s.reduce_rows.values())
-    copies = (
-        Gather.copies * len(s.gather_rows) + Reduce.copies * reduces + Total.copies + 6
-    )
+    reduces = 2 * s.panels + 1 + len(s.last_blocks)
+    copies = Gather.copies * len(s.gather_blocks) + Reduce.copies * reduces + Total.copies + 6
     small = pltpu.VMEM((8, 128), f32)
     scratch = [
         pltpu.VMEM((4, 2, 2, s.rows, width), bf16),
@@ -1220,8 +1271,11 @@
         pltpu.VMEM((4, 8, 128), f32),
         pltpu.SemaphoreType.DMA((copies,)),
         pltpu.SemaphoreType.DMA((copies,)),
-        pltpu.SemaphoreType.DMA((len(s.gather_rows) + 2,)),
-    ] + reduce_scratch(s.rows, s.cut, width)
+        pltpu.SemaphoreType.DMA((len(s.gather_blocks) + 2,)),
+        pltpu.VMEM((both, 128), f32),
+        pltpu.VMEM((4, 2, s.rows, width), bf16),
+        pltpu.VMEM((8, s.rows, width), bf16),
+    ]
     return pl.pallas_call(
         functools.partial(layer_kernel, s),
         out_shape=[
@@ -1230,13 +1284,13 @@
             jax.ShapeDtypeStruct((span, width), f32),
             jax.ShapeDtypeStruct((s.rows, width), bf16),
         ],
-        in_specs=[anywhere, anywhere, anywhere, vmem, vmem, smem, smem],
+        in_specs=[anywhere, anywhere, anywhere, vmem, smem, smem],
         out_specs=[anywhere, vmem, anywhere, vmem],
         scratch_shapes=scratch,
         compiler_params=pltpu.CompilerParams(
             collective_id=0, has_side_effects=True, vmem_limit_bytes=s.vmem
         ),
-    )(tokens, packed, teacher, order_row, order_col, length, valid)
+    )(tokens, packed, teacher, order_row, length, valid)
 
 
 def fused_shards(
@@ -1262,22 +1316,16 @@
     s = Sizes(span, width, ff, shard, w_down.shape[0], seq_len * dp_count)
     s.vmem = 63 * MIB
     gain_rows = jnp.pad(jnp.stack([gain_attn, gain_ffn]), ((0, 14), (0, width - shard)))
-    up_rows = jnp.transpose(w_up.reshape(shard, s.panels, width), (1, 0, 2)).reshape(-1, width)
+    up_rows = jnp.transpose(
+        w_up.reshape(shard, dp_count, s.panels, shard), (2, 0, 1, 3)
+    ).reshape(-1, width)
     packed = jnp.concatenate([w_query, w_key, w_value, w_out, gain_rows, up_rows, w_down])
-    order = tok_perm[0]
     ordered, total, token_grad, grads = layer(
-        s,
-        tokens[0],
-        packed,
-        teacher[0],
-        jnp.broadcast_to(order[None, :], (8, seq_len)),
-        jnp.broadcast_to(order[:, None], (seq_len, 128)),
-        seq_lengths,
-        valid_count,
+        s, tokens[0], packed, teacher[0], tok_perm, seq_lengths, valid_count
     )
     loss = (total[0, 0] / (2.0 * width * valid_count[0].astype(f32))).reshape(1)
     grads = grads.astype(f32)
-    up = grads[s.up0 : s.down0].reshape(s.panels, shard, width)
+    up = grads[s.up0 : s.down0].reshape(s.panels, shard, dp_count, shard)
     return (
         ordered[None],
         loss,
@@ -1286,7 +1334,7 @@
         grads[shard : 2 * shard],
         grads[2 * shard : 3 * shard],
         grads[s.out0 : s.gain0],
-        jnp.transpose(up, (1, 0, 2)).reshape(shard, ff),
+        jnp.transpose(up, (1, 2, 0, 3)).reshape(shard, ff),
         grads[s.down0 :],
         grads[s.gain0, :shard],
         grads[s.gain0 + 1, :shard],

time: 270 us -> 229 us (0.85); the launches traced: 270 us -> 226 us
  Pallas kernels: 249 us -> 206 us
    pallas_call x1, Pallas kernels: 249 us -> 206 us  [layer(): pl.pallas_call(functools.partial(layer_kernel, s), out_shape=[jax.ShapeDt...]
    reshape x2 -> x5, local copies, waits for them, and re-layouts: 1.85 us -> 6.01 us  [the longest x1 2.65 us: fused_shards(): jnp.transpose(up, (1, 2, 0, 3)).reshape(shard, ff)]
    broadcast_in_dim x2 -> x0, local copies, waits for them, and re-layouts: 3.03 us -> none  [the longest x1 1.73 us: fused_shards(): jnp.broadcast_to(order[:, None], (seq_len, 128))]
    unnamed x17 -> x27, local copies, waits for them, and re-layouts: 5.89 us -> 4.25 us
where the time goes in v3:
time: 229 us; the launch traced here: 226 us
  Pallas kernels  206 us (90%)
  local copies, waits for them, and re-layouts  15.8 us (7%)
  between operations  4.14 us (2%)
    pallas_call x1, Pallas kernels, layer(): pl.pallas_call(functools.partial(layer_kernel, s), out_shape=[jax.ShapeDt...  206 us

profile of v3, /device:TPU:0, one launch (start us, length us, event | category | flops | bytes accessed | tf_op | source)
XLA Modules:
  0.0 225.9 jit_solution(5499305591197699465)
XLA Ops:
  1.9 1.7 reshape.40
  3.7 0.0 copy-start.4
  3.7 0.0 copy-start.5
  3.7 0.0 copy-start.6
  3.7 0.0 copy-start.7
  3.7 0.0 copy-start.8
  3.7 0.0 copy-start.9
  3.7 0.0 copy-start.3
  3.8 0.1 copy.27
  3.9 0.8 reshape.41
  4.6 0.0 copy-done.4
  4.7 0.0 copy-done.5
  4.7 0.0 copy-done.6
  4.7 0.0 copy-done.7
  4.7 0.0 copy-done.8
  4.7 0.0 copy-done.9
  4.8 0.0 copy-done.3
  4.9 0.0 copy-start.2
  4.9 0.9 copy-done.2
  5.8 205.9 %shard_map.212 = (bf16[512,768]{1,0:T(8,128)(2,1)}, f32[8,128]{1,0:T(8,128)}, f32[512,768]{1,0:T(8,128)}, bf16[592,768]{1,0:T(8,128)(2,1)}) custom-call(bf16[512,768]{1,0:T(8,128)(2,1)} %bitcast.23, bf16[592,768]{1,0:T(8,128)(2,1)} %copy-done.2, bf16[512,768]{1,0:T(8,128)(2,1)} %bitcast.24, s32[1,1024]{1,0:T(1,128)} %refs_3_.1, s32[1]{0:T(128)S(6)} %copy.36.refs_4_, ...), custom_call_target="tpu_custom_call" | custom-call | tf_op jit(solution)/shard_map/pallas_call | solution.py:1279
  211.6 0.0 copy-start
  211.6 1.3 slice.27
  213.6 1.8 fusion.8
  215.4 0.0 copy-done
  215.4 0.9 fusion.7
  216.3 0.1 convert_element_type.10
  216.4 0.5 slice_bitcast_fusion
  216.9 0.8 reshape.43
  217.7 1.0 copy.25
  218.7 0.0 copy-start.1
  218.8 2.6 %reshape.44 = f32[48,3072]{1,0:T(8,128)} reshape(f32[48,16,4,48]{3,2,1,0:T(4,128)S(1)} %copy.25) | data formatting | bytes 1179648 | tf_op jit(solution)/shard_map/reshape | solution.py:1337
  221.4 2.1 copy.38
  223.5 0.0 copy-done.1
  223.5 1.1 copy.39
  (7 shorter events, 0.1 us)
Async XLA Ops:
  3.7 1.0 copy-start.4
  3.7 1.0 copy-start.5
  3.7 1.0 copy-start.6
  3.7 1.0 copy-start.7
  3.7 1.0 copy-start.8
  3.7 1.0 copy-start.9
  3.7 1.1 copy-start.3
  4.9 0.9 copy-start.2
  211.6 3.8 %copy-start = (bf16[592,768]{1,0:T(8,128)(2,1)S(1)}, bf16[592,768]{1,0:T(8,128)(2,1)}, u32[]{:S(2)}) copy-start(bf16[592,768]{1,0:T(8,128)(2,1)} %get-tuple-element.18) | copy-start | bytes 2727940
  218.7 4.7 %copy-start.1 = (f32[512,768]{1,0:T(8,128)S(1)}, f32[512,768]{1,0:T(8,128)}, u32[]{:S(2)}) copy-start(f32[512,768]{1,0:T(8,128)} %get-tuple-element.17) | copy-start | bytes 4718596
